TPU v7x, 32 devices: a whole 2x2x4 slice. The times are simulated.
32 devices in a mesh: scen: 4 (over z), net: 8 (over y, x, core).
Axes of the slice: x: 2, y: 2, z: 4, core: 2. Of those that a mesh axis runs over, the one named last changes fastest.
Arguments:
- coupling: bfloat16 [768, 64, 320], P('net'), may hold values from -0.3125 to 0.3125
- tie_blocks: bfloat16 [1024, 64, 128], P('net'), may hold values from -0.5 to 0.5
- w_pattern: int32 [768, 4], P('net'), may hold values from 0 to 127
- link_pattern: int32 [768], P('net'), may hold values from 0 to 127
- left_bounds: int32 [1024], P('net'), may hold values from 0 to 127
- right_bounds: int32 [1024], P('net'), may hold values from 0 to 127
- block_counts: int32 [8], P('net'), may hold values from 48 to 96, as said below
- commit_cost: float32 [1024, 64], P('net'), may hold values from -3 to 3
- dispatch_cost: float32 [1024, 64], P('net'), may hold values from -6 to 6
- demand: float32 [768, 64], P('net'), may hold values from -6 to 6
- wind_error: bfloat16 [768, 64, 512], P('net', None, 'scen'), may hold values from -3 to 3
- commit_start: float32 [1024, 64], P('net'), may hold values from 0 to 1
- dispatch_start: float32 [1024, 64, 512], P('net', None, 'scen'), may hold values from 0 to 2
- dual_start: float32 [768, 64, 512], P('net', None, 'scen'), may hold values from -8 to 8
- tie_start: float32 [1024, 64, 512], P('net', None, 'scen'), may hold values from -6 to 6
Outputs:
- commit_out: float32 [1024, 64], P('net')
- dispatch_out: float32 [1024, 64, 512], P('net', None, 'scen')
- dual_out: float32 [768, 64, 512], P('net', None, 'scen')
- tie_out: float32 [1024, 64, 512], P('net', None, 'scen')
Inputs may be any that keep to these rules, and one draw needn't show every extreme that they name: `block_counts`: some partition has all 96 row blocks active.
All inputs are finite; a program needn't handle non-finite values.
Results may differ from a plain program's by a relative error of at most 0.0035.
Values may be sent and summed in bfloat16 or wider, within the bound.
A program may use at most 192 MiB of HBM per device.

v0:
```python
import jax
import jax.numpy as jnp
from jax import lax
from jax.experimental import pallas as pl
from jax.experimental.pallas import tpu as pltpu
from jax.sharding import PartitionSpec as P

BLK = 64
KW = 4
ITERS = 2
UNROLL = 32
STEPS = 4

primal_step = 0.4
first_step = 1.0
dual_step = 0.4

VMEM = pl.BlockSpec(memory_space=pltpu.VMEM)
SMEM = pl.BlockSpec(memory_space=pltpu.SMEM)
F32 = jnp.float32
BF16 = jnp.bfloat16


def from_behind(value, axis, by):
    devices = lax.axis_size(axis)
    pairs = [(i, i + by) for i in range(devices) if 0 <= i + by < devices]
    return lax.ppermute(value, axis, pairs)


def sum_over_scen(value):
    devices = lax.axis_size("scen")
    total = value.astype(F32)
    for by in range(1, devices):
        pairs = [(i, (i + by) % devices) for i in range(devices)]
        total = total + lax.ppermute(value, "scen", pairs).astype(F32)
    return total


def per_step(shape):
    return pl.BlockSpec((shape[0] // STEPS,) + shape[1:], lambda i: (i, 0, 0))


def resident(shape):
    return pl.BlockSpec(shape, lambda i: (0, 0, 0))


def stepped_call(kernel, out_shape, in_specs, out_specs, flops, moved):
    return pl.pallas_call(
        kernel,
        grid=(STEPS,),
        out_shape=out_shape,
        in_specs=in_specs,
        out_specs=out_specs,
        compiler_params=pltpu.CompilerParams(vmem_limit_bytes=48 * 2**20),
        cost_estimate=pl.CostEstimate(flops=flops, bytes_accessed=moved, transcendentals=0),
    )


def rows_loop(count, step, unroll=UNROLL):
    unroll = max(u for u in range(1, unroll + 1) if count % u == 0)

    def chunk(c, carry):
        step([c * unroll + u for u in range(unroll)])
        return carry

    lax.fori_loop(0, count // unroll, chunk, 0)


def transposed_dot(a, b):
    return lax.dot_general(a, b, (((0,), (0,)), ((), ())), preferred_element_type=F32)


def zero_first(*refs):
    @pl.when(pl.program_id(0) == 0)
    def _():
        for ref in refs:
            ref[...] = jnp.zeros_like(ref)


def start_terms_kernel(live, right, tie, mu, terms, own):
    base = pl.program_id(0) * tie.shape[0]
    zero_first(own)

    def step(rows):
        parts = [transposed_dot(tie[j], (mu[j] * live[0]).astype(BF16)) for j in rows]
        for j, part in zip(rows, parts):
            terms[j] = part[BLK:].astype(BF16)
        for j, part in zip(rows, parts):
            own[right[base + j]] += part[:BLK]

    rows_loop(tie.shape[0], step)


def recourse_kernel(count, pattern, link, coupling, lam, grad, grad_first):
    base = pl.program_id(0) * coupling.shape[0]
    zero_first(grad, grad_first)

    def step(rows):
        halves = [jnp.where(base + r < count[0], lam[r], 0.0).astype(BF16) for r in rows]
        parts = [transposed_dot(coupling[r], h) for r, h in zip(rows, halves)]
        for r, part in zip(rows, parts):
            for k in range(KW):
                grad[pattern[(base + r) * KW + k]] += part[k * BLK : (k + 1) * BLK]
            grad_first[link[base + r]] += part[KW * BLK :]

    rows_loop(coupling.shape[0], step)


def primal_kernel(left, received, grad, own, cost, second, second_next, second_bar, sent, total):
    total[...] = grad[...] + own[...]

    def add_step(rows):
        for j in rows:
            total[left[j]] += received[j].astype(F32)

    rows_loop(received.shape[0], add_step, 8)

    def move_step(rows):
        news = []
        for b in rows:
            now = second[b]
            new = jnp.maximum(now - primal_step * (cost[b] - total[b]), 0.0)
            news.append((new, (2.0 * new - now).astype(BF16)))
        for b, (new, bar) in zip(rows, news):
            second_next[b] = new
            second_bar[b] = bar

    rows_loop(second.shape[0], move_step, 8)

    def gather_step(rows):
        picked = [second_bar[left[j]] for j in rows]
        for j, block in zip(rows, picked):
            sent[j] = block

    rows_loop(received.shape[0], gather_step, 16)


def dual_kernel(count, pattern, link, coupling, bar, first, target, lam, lam_next):
    base = pl.program_id(0) * coupling.shape[0]

    def step(rows):
        news = []
        for r in rows:
            at = base + r
            gathered = [bar[pattern[at * KW + k]] for k in range(KW)] + [first[link[at]]]
            coupled = jnp.dot(coupling[r], jnp.concatenate(gathered, axis=0), preferred_element_type=F32)
            new = lam[r] + dual_step * (target[r] - coupled)
            news.append(jnp.where(at < count[0], new, 0.0))
        for r, new in zip(rows, news):
            lam_next[r] = new

    rows_loop(coupling.shape[0], step)


def tie_kernel(live, right, tie, bar, arrived, mu, mu_next, *more):
    base = pl.program_id(0) * tie.shape[0]
    if more:
        zero_first(more[1])

    def step(rows):
        news = []
        for j in rows:
            stacked = jnp.concatenate([bar[right[base + j]], arrived[j]], axis=0)
            product = jnp.dot(tie[j], stacked, preferred_element_type=F32)
            news.append((mu[j] - dual_step * product) * live[0])
        parts = [transposed_dot(tie[j], new.astype(BF16)) for j, new in zip(rows, news)] if more else []
        for j, new in zip(rows, news):
            mu_next[j] = new
        for j, part in zip(rows, parts):
            more[0][j] = part[BLK:].astype(BF16)
            more[1][right[base + j]] += part[:BLK]

    rows_loop(tie.shape[0], step)


def primal_call(left, received, grad, own, cost, second):
    shape = second.shape
    return pl.pallas_call(
        primal_kernel,
        out_shape=(
            jax.ShapeDtypeStruct(shape, F32),
            jax.ShapeDtypeStruct(shape, BF16),
            jax.ShapeDtypeStruct(received.shape, BF16),
        ),
        in_specs=[SMEM] + [VMEM] * 5,
        out_specs=(VMEM,) * 3,
        scratch_shapes=[pltpu.VMEM(shape, F32)],
        compiler_params=pltpu.CompilerParams(vmem_limit_bytes=48 * 2**20),
        cost_estimate=pl.CostEstimate(flops=10**7, bytes_accessed=25 * 10**6, transcendentals=0),
    )(left, received, grad, own, cost, second)


def body(
    coupling,
    tie_blocks,
    w_pattern,
    link_pattern,
    left_bounds,
    right_bounds,
    block_counts,
    commit_cost,
    dispatch_cost,
    demand,
    wind_error,
    commit_start,
    dispatch_start,
    dual_start,
    tie_start,
):
    scen_dev = dispatch_start.shape[2]
    scen_total = scen_dev * lax.axis_size("scen")
    second_shape = dispatch_start.shape
    tie_shape = tie_start.shape
    wide_shape = commit_start.shape + (scen_dev,)
    live = (lax.axis_index("net") < lax.axis_size("net") - 1).astype(F32).reshape(1)
    pattern = w_pattern.reshape(-1)
    cost = jnp.broadcast_to(dispatch_cost[:, :, None], second_shape)
    target = demand[:, :, None] + wind_error.astype(F32)
    first_now = commit_start
    second_now = dispatch_start
    dual_now = dual_start
    tie_now = tie_start
    second_f32 = jax.ShapeDtypeStruct(second_shape, F32)
    tie_f32 = jax.ShapeDtypeStruct(tie_shape, F32)
    tie_bf16 = jax.ShapeDtypeStruct(tie_shape, BF16)
    dual_f32 = jax.ShapeDtypeStruct(dual_start.shape, F32)
    ties, rows = per_step(tie_shape), per_step(dual_start.shape)
    tie_mats, row_mats = per_step(tie_blocks.shape), per_step(coupling.shape)
    seconds, wides = resident(second_shape), resident(wide_shape)
    terms, own = stepped_call(
        start_terms_kernel,
        (tie_bf16, second_f32),
        [SMEM, SMEM, tie_mats, ties],
        (ties, seconds),
        3 * 10**8,
        13 * 10**6,
    )(live, right_bounds, tie_blocks, tie_start)
    for iteration in range(ITERS):
        received = from_behind(terms, "net", 1)
        grad, grad_wide = stepped_call(
            recourse_kernel,
            (second_f32, jax.ShapeDtypeStruct(wide_shape, F32)),
            [SMEM] * 3 + [row_mats, rows],
            (seconds, wides),
            5 * 10**8,
            16 * 10**6,
        )(block_counts, pattern, link_pattern, coupling, dual_now)
        grad_first = sum_over_scen((jnp.sum(grad_wide, axis=2) / scen_total).astype(BF16))
        second_next, second_bar, sent = primal_call(left_bounds, received, grad, own, cost, second_now)
        sent, grad_first = lax.optimization_barrier((sent, grad_first))
        arrived = from_behind(sent, "net", -1)
        first_next = jnp.clip(first_now - first_step * (commit_cost - grad_first), 0.0, 1.0)
        first_bar = (2.0 * first_next - first_now).astype(BF16)
        first_wide = jnp.broadcast_to(first_bar[:, :, None], wide_shape)
        dual_now = stepped_call(
            dual_kernel,
            dual_f32,
            [SMEM] * 3 + [row_mats, seconds, wides, rows, rows],
            rows,
            5 * 10**8,
            18 * 10**6,
        )(block_counts, pattern, link_pattern, coupling, second_bar, first_wide, target, dual_now)
        arrived, dual_now = lax.optimization_barrier((arrived, dual_now))
        more = iteration < ITERS - 1
        got = stepped_call(
            tie_kernel,
            (tie_f32, tie_bf16, second_f32) if more else (tie_f32,),
            [SMEM, SMEM, tie_mats, seconds, ties, ties],
            (ties, ties, seconds) if more else (ties,),
            6 * 10**8,
            18 * 10**6,
        )(live, right_bounds, tie_blocks, second_bar, arrived, tie_now)
        tie_now = got[0]
        if more:
            terms, own = got[1:]
        first_now = first_next
        second_now = second_next
    return (first_now, second_now, dual_now, tie_now)


def solution(mesh):
    return jax.shard_map(
        body,
        mesh=mesh,
        in_specs=(
            P("net", None, None),
            P("net", None, None),
            P("net", None),
            P("net"),
            P("net"),
            P("net"),
            P("net"),
            P("net", None),
            P("net", None),
            P("net", None),
            P("net", None, "scen"),
            P("net", None),
            P("net", None, "scen"),
            P("net", None, "scen"),
            P("net", None, "scen"),
        ),
        out_specs=(
            P("net", None),
            P("net", None, "scen"),
            P("net", None, "scen"),
            P("net", None, "scen"),
        ),
        check_vma=False,
    )
```

profile of v0, /device:TPU:1, one launch (start us, length us, event | category | flops | bytes accessed | tf_op | source)
XLA Modules:
  0.0 161.7 jit_solution(1625653569355367305)
XLA Ops:
  0.7 1.6 copy-done.1
  2.9 6.9 %shard_map.174 = (bf16[128,64,128]{2,1,0:T(8,128)(2,1)}, f32[128,64,128]{2,1,0:T(8,128)}) custom-call(f32[1]{0:T(128)} %bitcast.live, s32[128]{0:T(128)S(1)} %copy-done.7, bf16[128,64,128]{2,1,0:T(8,128)(2,1)S(1)} %copy-done.1, f32[128,64,128]{2,1,0:T(8,128)} %mu.3), custom_call_target="tpu_custom_call" | custom-call | flops 300000000 | bytes 13000000 | tf_op jit(solution)/shard_map/pallas_call | solution.py:230
  9.8 4.5 %collective-permute-start = (bf16[128,64,128]{2,1,0:T(8,128)(2,1)}, bf16[128,64,128]{2,1,0:T(8,128)(2,1)}, u32[]{:S(2)}, u32[]{:S(2)}) collective-permute-start(bf16[128,64,128]{2,1,0:T(8,128)(2,1)} %get-tuple-element.27), channel_id=1, source_target_pairs={{0,1},{1,2},{2,3},{3,4},{4,5},{5,6},{6,7},{8,9},{9,10},{10,11},{11... | collective-permute-start | bytes 6291464 | tf_op jit(solution)/shard_map/ppermute | solution.py:27
  15.2 9.3 %shard_map.175 = (f32[128,64,128]{2,1,0:T(8,128)}, f32[128,64,128]{2,1,0:T(8,128)}) custom-call(s32[1]{0:T(128)S(6)} %copy.36.count, s32[384]{0:T(512)S(1)} %reshape.22.pattern, s32[96]{0:T(128)S(1)} %copy-done.6, bf16[96,64,320]{2,1,0:T(8,128)(2,1)} %coupling.7, f32[96,64,128]{2,1,0:T(8,128)S(1)} %copy-done.4), custom_call_target="tpu_custom_call" | custom-call | flops 500000000 | bytes 16000000 | tf_op jit(solution)/shard_map/pallas_call | solution.py:240
  24.5 3.3 %reduce_sum.18 = f32[128,64]{1,0:T(8,128)S(1)} reduce(f32[128,64,128]{2,1,0:T(8,128)} %get-tuple-element.31, f32[]{:T(128)} %constant.6.clone.1), dimensions={2}, to_apply=%region_0.0 | reduce | flops 1040384 | bytes 4227076 | tf_op jit(solution)/shard_map/reduce_sum | solution.py:248
  27.9 1.4 collective-permute-start.1
  29.2 2.3 %collective-permute-start.2 = (bf16[128,64]{1,0:T(8,128)(2,1)S(1)}, bf16[128,64]{1,0:T(8,128)(2,1)S(1)}, u32[]{:S(2)}, u32[]{:S(2)}) collective-permute-start(bf16[128,64]{1,0:T(8,128)(2,1)S(1)} %multiply_convert_fusion.1), channel_id=1, source_target_pairs={{0,16},{8,24},{16,0},{24,8},{1,17},{9,25},{17,1},{25,9},{2,18},{10... | collective-permute-start | bytes 49160 | tf_op jit(solution)/shard_map/ppermute | solution.py:35
  31.5 1.1 collective-permute-start.3
  34.4 3.3 %collective-permute-done.received = bf16[128,64,128]{2,1,0:T(8,128)(2,1)} collective-permute-done((bf16[128,64,128]{2,1,0:T(8,128)(2,1)}, bf16[128,64,128]{2,1,0:T(8,128)(2,1)}, u32[]{:S(2)}, u32[]{:S(2)}) %collective-permute-start) | collective-permute-done | bytes 2097184 | tf_op jit(solution)/shard_map/ppermute | solution.py:27
  37.6 2.6 %broadcast_in_dim.6.cost = f32[128,64,128]{2,1,0:T(8,128)} broadcast(f32[128,64]{1,0:T(8,128)S(1)} %copy.29), dimensions={0,1} | broadcast | bytes 4227072 | tf_op jit(solution)/shard_map/broadcast_in_dim | solution.py:217
  40.2 11.4 %shard_map.176 = (f32[128,64,128]{2,1,0:T(8,128)}, bf16[128,64,128]{2,1,0:T(8,128)(2,1)S(1)}, bf16[128,64,128]{2,1,0:T(8,128)(2,1)}) custom-call(s32[128]{0:T(128)S(1)} %copy-done.9, bf16[128,64,128]{2,1,0:T(8,128)(2,1)} %collective-permute-done.received, f32[128,64,128]{2,1,0:T(8,128)} %get-tuple-element.28.grad, f32[128,64,128]{2,1,0:T(8,128)} %get-tuple-element.29.own, ...), custom_call_target="tpu_custom_call" | custom-call | flops 10000000 | bytes 25000000 | tf_op jit(solution)/shard_map/pallas_call | solution.py:178
  51.6 1.9 %collective-permute-start.4 = (bf16[128,64,128]{2,1,0:T(8,128)(2,1)}, bf16[128,64,128]{2,1,0:T(8,128)(2,1)}, u32[]{:S(2)}, u32[]{:S(2)}) collective-permute-start(bf16[128,64,128]{2,1,0:T(8,128)(2,1)} %get-tuple-element.34), channel_id=1, source_target_pairs={{1,0},{2,1},{3,2},{4,3},{5,4},{6,5},{7,6},{9,8},{10,9},{11,10},{12... | collective-permute-start | bytes 6291464 | tf_op jit(solution)/shard_map/ppermute | solution.py:27
  53.8 3.3 %convert_add_fusion.target = f32[96,64,128]{2,1,0:T(8,128)} fusion(bf16[96,64,128]{2,1,0:T(8,128)(2,1)} %param.25, f32[96,64]{1,0:T(8,128)S(1)} %copy.33), kind=kLoop, calls=%fused_computation | loop fusion | flops 1572864 | bytes 4743168 | tf_op jit(solution)/shard_map/add | solution.py:218
  57.1 1.6 %broadcast_in_dim.7.first = bf16[128,64,128]{2,1,0:T(8,128)(2,1)S(1)} broadcast(bf16[128,64]{1,0:T(8,128)(2,1)S(1)} %subtract_convert_fusion.1), dimensions={0,1} | broadcast | bytes 2113536 | tf_op jit(solution)/shard_map/broadcast_in_dim | solution.py:254
  58.8 7.1 %shard_map.177.lam = f32[96,64,128]{2,1,0:T(8,128)} custom-call(s32[1]{0:T(128)S(6)} %copy.36.count, s32[384]{0:T(512)S(1)} %reshape.22.pattern, s32[96]{0:T(128)S(1)} %copy-done.6, bf16[96,64,320]{2,1,0:T(8,128)(2,1)} %coupling.7, bf16[128,64,128]{2,1,0:T(8,128)(2,1)S(1)} %get-tuple-element.33.bar, bf16[128,64,128]{2,1,0:T(8,128)(2,1)S(1)} %broadcast_in_dim.7.first, ...), custom_call_target="tpu_custom_call" | custom-call | flops 500000000 | bytes 18000000 | tf_op jit(solution)/shard_map/pallas_call | solution.py:255
  65.9 14.1 %collective-permute-done.4.arrived = bf16[128,64,128]{2,1,0:T(8,128)(2,1)} collective-permute-done((bf16[128,64,128]{2,1,0:T(8,128)(2,1)}, bf16[128,64,128]{2,1,0:T(8,128)(2,1)}, u32[]{:S(2)}, u32[]{:S(2)}) %collective-permute-start.4) | collective-permute-done | bytes 2097184 | tf_op jit(solution)/shard_map/ppermute | solution.py:27
  80.0 9.5 %shard_map.178 = (f32[128,64,128]{2,1,0:T(8,128)}, bf16[128,64,128]{2,1,0:T(8,128)(2,1)}, f32[128,64,128]{2,1,0:T(8,128)}) custom-call(f32[1]{0:T(128)} %bitcast.live, s32[128]{0:T(128)S(1)} %copy-done.8, bf16[128,64,128]{2,1,0:T(8,128)(2,1)S(1)} %copy-done.2, bf16[128,64,128]{2,1,0:T(8,128)(2,1)} %copy-done.5, ...), custom_call_target="tpu_custom_call" | custom-call | flops 600000000 | bytes 18000000 | tf_op jit(solution)/shard_map/pallas_call | solution.py:265
  89.5 1.9 %collective-permute-start.5 = (bf16[128,64,128]{2,1,0:T(8,128)(2,1)}, bf16[128,64,128]{2,1,0:T(8,128)(2,1)S(1)}, u32[]{:S(2)}, u32[]{:S(2)}) collective-permute-start(bf16[128,64,128]{2,1,0:T(8,128)(2,1)} %get-tuple-element.36), channel_id=1, source_target_pairs={{0,1},{1,2},{2,3},{3,4},{4,5},{5,6},{6,7},{8,9},{9,10},{10,11},{11... | collective-permute-start | bytes 6291464 | tf_op jit(solution)/shard_map/ppermute | solution.py:27
  91.4 9.3 %shard_map.179 = (f32[128,64,128]{2,1,0:T(8,128)}, f32[128,64,128]{2,1,0:T(8,128)}) custom-call(s32[1]{0:T(128)S(6)} %copy.36.count, s32[384]{0:T(512)S(1)} %reshape.22.pattern, s32[96]{0:T(128)S(1)} %copy-done.6, bf16[96,64,320]{2,1,0:T(8,128)(2,1)} %coupling.7, f32[96,64,128]{2,1,0:T(8,128)S(1)} %copy-done), custom_call_target="tpu_custom_call" | custom-call | flops 500000000 | bytes 16000000 | tf_op jit(solution)/shard_map/pallas_call | solution.py:240
  100.7 3.3 %reduce_sum.19 = f32[128,64]{1,0:T(8,128)S(1)} reduce(f32[128,64,128]{2,1,0:T(8,128)} %get-tuple-element.42, f32[]{:T(128)} %constant.6.clone.1), dimensions={2}, to_apply=%region_1.2 | reduce | flops 1040384 | bytes 4227076 | tf_op jit(solution)/shard_map/reduce_sum | solution.py:248
  104.1 1.4 collective-permute-start.6
  105.4 2.3 %collective-permute-start.7 = (bf16[128,64]{1,0:T(8,128)(2,1)S(1)}, bf16[128,64]{1,0:T(8,128)(2,1)S(1)}, u32[]{:S(2)}, u32[]{:S(2)}) collective-permute-start(bf16[128,64]{1,0:T(8,128)(2,1)S(1)} %multiply_convert_fusion), channel_id=1, source_target_pairs={{0,16},{8,24},{16,0},{24,8},{1,17},{9,25},{17,1},{25,9},{2,18},{10... | collective-permute-start | bytes 49160 | tf_op jit(solution)/shard_map/ppermute | solution.py:35
  107.7 1.1 collective-permute-start.8
  109.1 2.0 %collective-permute-done.8 = bf16[128,64]{1,0:T(8,128)(2,1)S(1)} collective-permute-done((bf16[128,64]{1,0:T(8,128)(2,1)S(1)}, bf16[128,64]{1,0:T(8,128)(2,1)S(1)}, u32[]{:S(2)}, u32[]{:S(2)}) %collective-permute-start.8) | collective-permute-done | bytes 16416 | tf_op jit(solution)/shard_map/ppermute | solution.py:35
  111.1 3.6 %collective-permute-done.5.received = bf16[128,64,128]{2,1,0:T(8,128)(2,1)S(1)} collective-permute-done((bf16[128,64,128]{2,1,0:T(8,128)(2,1)}, bf16[128,64,128]{2,1,0:T(8,128)(2,1)S(1)}, u32[]{:S(2)}, u32[]{:S(2)}) %collective-permute-start.5) | collective-permute-done | bytes 2097184 | tf_op jit(solution)/shard_map/ppermute | solution.py:27
  114.7 1.3 copy-done.10
  116.0 11.4 %shard_map.180 = (f32[128,64,128]{2,1,0:T(8,128)}, bf16[128,64,128]{2,1,0:T(8,128)(2,1)S(1)}, bf16[128,64,128]{2,1,0:T(8,128)(2,1)}) custom-call(s32[128]{0:T(128)S(1)} %copy-done.9, bf16[128,64,128]{2,1,0:T(8,128)(2,1)} %copy-done.10, f32[128,64,128]{2,1,0:T(8,128)} %get-tuple-element.38.grad, f32[128,64,128]{2,1,0:T(8,128)} %get-tuple-element.39.own, ...), custom_call_target="tpu_custom_call" | custom-call | flops 10000000 | bytes 25000000 | tf_op jit(solution)/shard_map/pallas_call | solution.py:178
  127.5 1.9 %collective-permute-start.9 = (bf16[128,64,128]{2,1,0:T(8,128)(2,1)}, bf16[128,64,128]{2,1,0:T(8,128)(2,1)}, u32[]{:S(2)}, u32[]{:S(2)}) collective-permute-start(bf16[128,64,128]{2,1,0:T(8,128)(2,1)} %get-tuple-element.45), channel_id=1, source_target_pairs={{1,0},{2,1},{3,2},{4,3},{5,4},{6,5},{7,6},{9,8},{10,9},{11,10},{12... | collective-permute-start | bytes 6291464 | tf_op jit(solution)/shard_map/ppermute | solution.py:27
  130.1 1.6 broadcast_in_dim.8.first
  131.7 7.1 %shard_map.181 = f32[96,64,128]{2,1,0:T(8,128)} custom-call(s32[1]{0:T(128)S(6)} %copy.36.count, s32[384]{0:T(512)S(1)} %reshape.22.pattern, s32[96]{0:T(128)S(1)} %copy-done.6, bf16[96,64,320]{2,1,0:T(8,128)(2,1)} %coupling.7, bf16[128,64,128]{2,1,0:T(8,128)(2,1)S(1)} %get-tuple-element.46.bar, bf16[128,64,128]{2,1,0:T(8,128)(2,1)S(1)} %broadcast_in_dim.8.first, ...), custom_call_target="tpu_custom_call" | custom-call | flops 500000000 | bytes 18000000 | tf_op jit(solution)/shard_map/pallas_call | solution.py:255
  138.9 16.9 %collective-permute-done.9.arrived = bf16[128,64,128]{2,1,0:T(8,128)(2,1)} collective-permute-done((bf16[128,64,128]{2,1,0:T(8,128)(2,1)}, bf16[128,64,128]{2,1,0:T(8,128)(2,1)}, u32[]{:S(2)}, u32[]{:S(2)}) %collective-permute-start.9) | collective-permute-done | bytes 2097184 | tf_op jit(solution)/shard_map/ppermute | solution.py:27
  155.8 5.9 %shard_map.182 = f32[128,64,128]{2,1,0:T(8,128)} custom-call(f32[1]{0:T(128)} %bitcast.live, s32[128]{0:T(128)S(1)} %copy-done.8, bf16[128,64,128]{2,1,0:T(8,128)(2,1)S(1)} %copy-done.3, bf16[128,64,128]{2,1,0:T(8,128)(2,1)S(1)} %get-tuple-element.46.bar, bf16[128,64,128]{2,1,0:T(8,128)(2,1)} %collective-permute-done.9.arrived, ...), custom_call_target="tpu_custom_call" | custom-call | flops 600000000 | bytes 18000000 | tf_op jit(solution)/shard_map/pallas_call | solution.py:265
  (48 shorter events, 4.0 us)
Async XLA Ops:
  0.6 1.6 copy-start.1
  2.2 0.7 copy-start.7
  2.9 11.4 %copy-start.15 = (s32[96,4]{0,1:T(4,128)S(1)}, s32[96,4]{0,1:T(4,128)}, u32[]{:S(2)}) copy-start(s32[96,4]{0,1:T(4,128)} %param.17) | copy-start | bytes 4612
  2.9 12.3 %copy-start.4 = (f32[96,64,128]{2,1,0:T(8,128)S(1)}, f32[96,64,128]{2,1,0:T(8,128)}, u32[]{:S(2)}) copy-start(f32[96,64,128]{2,1,0:T(8,128)} %lam.3) | copy-start | bytes 9437188
  2.9 12.3 %copy-start.6 = (s32[96]{0:T(128)S(1)}, s32[96]{0:T(128)}, u32[]{:S(2)}) copy-start(s32[96]{0:T(128)} %link.7) | copy-start | bytes 1156
  9.8 27.8 %collective-permute-start = (bf16[128,64,128]{2,1,0:T(8,128)(2,1)}, bf16[128,64,128]{2,1,0:T(8,128)(2,1)}, u32[]{:S(2)}, u32[]{:S(2)}) collective-permute-start(bf16[128,64,128]{2,1,0:T(8,128)(2,1)} %get-tuple-element.27), channel_id=1, source_target_pairs={{0,1},{1,2},{2,3},{3,4},{4,5},{5,6},{6,7},{8,9},{9,10},{10,11},{11... | collective-permute-start | bytes 6291464 | tf_op jit(solution)/shard_map/ppermute | solution.py:27
  24.5 8.1 %copy-start.11 = (f32[128,64]{0,1:T(8,128)S(1)}, f32[128,64]{0,1:T(8,128)}, u32[]{:S(2)}) copy-start(f32[128,64]{0,1:T(8,128)} %param.23) | copy-start | bytes 98308
  27.9 12.3 %copy-start.9 = (s32[128]{0:T(128)S(1)}, s32[128]{0:T(128)}, u32[]{:S(2)}) copy-start(s32[128]{0:T(128)} %left.3) | copy-start | bytes 1540
  27.9 5.1 %collective-permute-start.1 = (bf16[128,64]{1,0:T(8,128)(2,1)S(1)}, bf16[128,64]{1,0:T(8,128)(2,1)S(1)}, u32[]{:S(2)}, u32[]{:S(2)}) collective-permute-start(bf16[128,64]{1,0:T(8,128)(2,1)S(1)} %multiply_convert_fusion.1), channel_id=1, source_target_pairs={{0,8},{8,16},{16,24},{24,0},{1,9},{9,17},{17,25},{25,1},{2,10},{10... | collective-permute-start | bytes 49160 | tf_op jit(solution)/shard_map/ppermute | solution.py:35
  29.2 4.0 %collective-permute-start.2 = (bf16[128,64]{1,0:T(8,128)(2,1)S(1)}, bf16[128,64]{1,0:T(8,128)(2,1)S(1)}, u32[]{:S(2)}, u32[]{:S(2)}) collective-permute-start(bf16[128,64]{1,0:T(8,128)(2,1)S(1)} %multiply_convert_fusion.1), channel_id=1, source_target_pairs={{0,16},{8,24},{16,0},{24,8},{1,17},{9,25},{17,1},{25,9},{2,18},{10... | collective-permute-start | bytes 49160 | tf_op jit(solution)/shard_map/ppermute | solution.py:35
  31.5 2.8 %collective-permute-start.3 = (bf16[128,64]{1,0:T(8,128)(2,1)S(1)}, bf16[128,64]{1,0:T(8,128)(2,1)S(1)}, u32[]{:S(2)}, u32[]{:S(2)}) collective-permute-start(bf16[128,64]{1,0:T(8,128)(2,1)S(1)} %multiply_convert_fusion.1), channel_id=1, source_target_pairs={{0,24},{8,0},{16,8},{24,16},{1,25},{9,1},{17,9},{25,17},{2,26},{10... | collective-permute-start | bytes 49160 | tf_op jit(solution)/shard_map/ppermute | solution.py:35
  40.2 13.3 %copy-start.12 = (f32[128,64]{0,1:T(8,128)S(1)}, f32[128,64]{0,1:T(8,128)}, u32[]{:S(2)}) copy-start(f32[128,64]{0,1:T(8,128)} %param.22) | copy-start | bytes 98308
  40.2 13.4 %copy-start.13 = (f32[128,64]{0,1:T(8,128)S(1)}, f32[128,64]{0,1:T(8,128)}, u32[]{:S(2)}) copy-start(f32[128,64]{0,1:T(8,128)} %param.26) | copy-start | bytes 98308
  40.2 13.5 %copy-start.14 = (f32[96,64]{0,1:T(8,128)S(1)}, f32[96,64]{0,1:T(8,128)}, u32[]{:S(2)}) copy-start(f32[96,64]{0,1:T(8,128)} %param.24) | copy-start | bytes 73732
  51.6 7.2 %copy-start.5 = (bf16[128,64,128]{2,1,0:T(8,128)(2,1)}, bf16[128,64,128]{2,1,0:T(8,128)(2,1)S(1)}, u32[]{:S(2)}) copy-start(bf16[128,64,128]{2,1,0:T(8,128)(2,1)S(1)} %get-tuple-element.33.bar) | copy-start | bytes 6291460
  51.6 28.4 %collective-permute-start.4 = (bf16[128,64,128]{2,1,0:T(8,128)(2,1)}, bf16[128,64,128]{2,1,0:T(8,128)(2,1)}, u32[]{:S(2)}, u32[]{:S(2)}) collective-permute-start(bf16[128,64,128]{2,1,0:T(8,128)(2,1)} %get-tuple-element.34), channel_id=1, source_target_pairs={{1,0},{2,1},{3,2},{4,3},{5,4},{6,5},{7,6},{9,8},{10,9},{11,10},{12... | collective-permute-start | bytes 6291464 | tf_op jit(solution)/shard_map/ppermute | solution.py:27
  58.7 21.3 %copy-start.2 = (bf16[128,64,128]{2,1,0:T(8,128)(2,1)S(1)}, bf16[128,64,128]{2,1,0:T(8,128)(2,1)}, u32[]{:S(2)}) copy-start(bf16[128,64,128]{2,1,0:T(8,128)(2,1)} %tie.5) | copy-start | bytes 6291460
  58.7 21.2 %copy-start.8 = (s32[128]{0:T(128)S(1)}, s32[128]{0:T(128)}, u32[]{:S(2)}) copy-start(s32[128]{0:T(128)} %right.5) | copy-start | bytes 1540
  65.9 25.5 %copy-start = (f32[96,64,128]{2,1,0:T(8,128)S(1)}, f32[96,64,128]{2,1,0:T(8,128)}, u32[]{:S(2)}) copy-start(f32[96,64,128]{2,1,0:T(8,128)} %shard_map.177.lam) | copy-start | bytes 9437188
  89.5 25.2 %collective-permute-start.5 = (bf16[128,64,128]{2,1,0:T(8,128)(2,1)}, bf16[128,64,128]{2,1,0:T(8,128)(2,1)S(1)}, u32[]{:S(2)}, u32[]{:S(2)}) collective-permute-start(bf16[128,64,128]{2,1,0:T(8,128)(2,1)} %get-tuple-element.36), channel_id=1, source_target_pairs={{0,1},{1,2},{2,3},{3,4},{4,5},{5,6},{6,7},{8,9},{9,10},{10,11},{11... | collective-permute-start | bytes 6291464 | tf_op jit(solution)/shard_map/ppermute | solution.py:27
  104.1 4.7 %collective-permute-start.6 = (bf16[128,64]{1,0:T(8,128)(2,1)S(1)}, bf16[128,64]{1,0:T(8,128)(2,1)S(1)}, u32[]{:S(2)}, u32[]{:S(2)}) collective-permute-start(bf16[128,64]{1,0:T(8,128)(2,1)S(1)} %multiply_convert_fusion), channel_id=1, source_target_pairs={{0,8},{8,16},{16,24},{24,0},{1,9},{9,17},{17,25},{25,1},{2,10},{10... | collective-permute-start | bytes 49160 | tf_op jit(solution)/shard_map/ppermute | solution.py:35
  105.4 3.7 %collective-permute-start.7 = (bf16[128,64]{1,0:T(8,128)(2,1)S(1)}, bf16[128,64]{1,0:T(8,128)(2,1)S(1)}, u32[]{:S(2)}, u32[]{:S(2)}) collective-permute-start(bf16[128,64]{1,0:T(8,128)(2,1)S(1)} %multiply_convert_fusion), channel_id=1, source_target_pairs={{0,16},{8,24},{16,0},{24,8},{1,17},{9,25},{17,1},{25,9},{2,18},{10... | collective-permute-start | bytes 49160 | tf_op jit(solution)/shard_map/ppermute | solution.py:35
  107.7 3.4 %collective-permute-start.8 = (bf16[128,64]{1,0:T(8,128)(2,1)S(1)}, bf16[128,64]{1,0:T(8,128)(2,1)S(1)}, u32[]{:S(2)}, u32[]{:S(2)}) collective-permute-start(bf16[128,64]{1,0:T(8,128)(2,1)S(1)} %multiply_convert_fusion), channel_id=1, source_target_pairs={{0,24},{8,0},{16,8},{24,16},{1,25},{9,1},{17,9},{25,17},{2,26},{10... | collective-permute-start | bytes 49160 | tf_op jit(solution)/shard_map/ppermute | solution.py:35
  114.7 1.3 copy-start.10
  127.5 28.3 %collective-permute-start.9 = (bf16[128,64,128]{2,1,0:T(8,128)(2,1)}, bf16[128,64,128]{2,1,0:T(8,128)(2,1)}, u32[]{:S(2)}, u32[]{:S(2)}) collective-permute-start(bf16[128,64,128]{2,1,0:T(8,128)(2,1)} %get-tuple-element.45), channel_id=1, source_target_pairs={{1,0},{2,1},{3,2},{4,3},{5,4},{6,5},{7,6},{9,8},{10,9},{11,10},{12... | collective-permute-start | bytes 6291464 | tf_op jit(solution)/shard_map/ppermute | solution.py:27
  131.7 24.0 %copy-start.3 = (bf16[128,64,128]{2,1,0:T(8,128)(2,1)S(1)}, bf16[128,64,128]{2,1,0:T(8,128)(2,1)}, u32[]{:S(2)}) copy-start(bf16[128,64,128]{2,1,0:T(8,128)(2,1)} %tie.5) | copy-start | bytes 6291460
where the time goes:
time: 163 us; the launch traced here: 162 us
  Pallas kernels  78 us (48%)
  waiting for transfers between devices  41.7 us (26%)
  starting transfers between devices  19.7 us (12%)
  local copies, waits for them, and re-layouts  10.7 us (7%)
  other arithmetic  10.1 us (6%)
    ppermute x4, waiting for transfers between devices, from_behind(): return lax.ppermute(value, axis, pairs)  37.8 us
    pallas_call x2, Pallas kernels, primal_call(): pl.pallas_call(primal_kernel, out_shape=(jax.ShapeDtypeStruct(shape, F32)...  22.8 us
    pallas_call x2, Pallas kernels, body(): stepped_call(recourse_kernel, (second_f32, jax.ShapeDtypeStruct(wide_shap...  18.5 us
    pallas_call x2, Pallas kernels, body(): stepped_call(tie_kernel, (tie_f32, tie_bf16, second_f32) if more else (ti...  15.4 us
    pallas_call x2, Pallas kernels, body(): stepped_call(dual_kernel, dual_f32, [SMEM] * 3 + [row_mats, seconds, wide...  14.3 us
    ppermute x4, starting transfers between devices, from_behind(): return lax.ppermute(value, axis, pairs)  10.2 us
    ppermute x6, starting transfers between devices, sum_over_scen(): total = total + lax.ppermute(value, 'scen', pairs).astype(F32)  9.45 us
    pallas_call x1, Pallas kernels, body(): stepped_call(start_terms_kernel, (tie_bf16, second_f32), [SMEM, SMEM, tie...  6.93 us
  transfers between devices with their start and end apart: 10, of which 9 were waited for; matrix products, arithmetic and copies ran while one was open for 9% of the time, Pallas kernels for 20%

commit v1 on v0

v1 whole, which is shorter than its diff:
```python
import functools

import jax
import jax.numpy as jnp
from jax import lax
from jax.experimental import pallas as pl
from jax.experimental.pallas import tpu as pltpu
from jax.sharding import PartitionSpec as P

BLK = 64
KW = 4
ITERS = 2
CHUNKS = 8
UNROLL = 16

primal_step = 0.4
first_step = 1.0
dual_step = 0.4

F32 = jnp.float32
BF16 = jnp.bfloat16
MESH = pl.DeviceIdType.MESH


def transposed_dot(a, b):
    return lax.dot_general(a, b, (((0,), (0,)), ((), ())), preferred_element_type=F32)


def spread(columns, at):
    return jnp.broadcast_to(columns[:, at : at + 1], columns.shape)


def loop(count, step, carry=0, unroll=UNROLL):
    unroll = max(u for u in range(1, unroll + 1) if count % u == 0)
    return lax.fori_loop(0, count // unroll, lambda c, state: step(c * unroll, unroll, state), carry)


def layout_of(rows, ties, blocks, slots):
    sizes = dict(
        count=1,
        pattern=rows * KW,
        link=rows,
        prev_rec=KW * rows,
        last_rec=KW * blocks,
        right=ties,
        prev_own=ties,
        last_own=blocks,
        prev_out=ties,
        last_out=slots,
        slot_of_tie=ties,
        slot_of_block=blocks,
        block_of_slot=slots,
    )
    offsets, at = {}, 0
    for name, size in sizes.items():
        offsets[name] = at
        at += size
    return offsets


def kernel(
    offsets,
    index,
    cost_t,
    demand_t,
    commit_cost_t,
    commit_t,
    coupling_hbm,
    tie_hbm,
    wind_hbm,
    second_hbm,
    lam_hbm,
    mu_hbm,
    commit_out,
    second_out,
    lam_out,
    mu_out,
    coupling,
    tie,
    wind,
    second,
    lam,
    mu,
    rec0,
    rec1,
    rec2,
    rec3,
    outs,
    own,
    send_terms,
    got_terms0,
    got_terms1,
    send_bar,
    got_bar0,
    got_bar1,
    bar,
    first_wide,
    first_t,
    send_first,
    got_first,
    load_sems,
    store_sems,
    terms_ssem,
    terms_rsem,
    bar_ssem,
    bar_rsem,
    first_ssem,
    first_rsem,
):
    recs = (rec0, rec1, rec2, rec3)
    got_terms, got_bar = (got_terms0, got_terms1), (got_bar0, got_bar1)
    me_s, me = lax.axis_index("scen"), lax.axis_index("net")
    scens, parts = lax.axis_size("scen"), lax.axis_size("net")
    rows, ties, blocks = lam.shape[0], mu.shape[0], second.shape[0]
    slots = send_terms.shape[0]
    scen_total = lam.shape[2] * scens
    has_next, has_prev = me < parts - 1, me > 0

    def at(name, i):
        return index[offsets[name] + i]

    loads = [
        pltpu.make_async_copy(src, dst, load_sems.at[i])
        for i, (src, dst) in enumerate(
            [(tie_hbm, tie), (mu_hbm, mu), (coupling_hbm, coupling), (lam_hbm, lam), (second_hbm, second), (wind_hbm, wind)]
        )
    ]
    for copy in loads:
        copy.start()

    entry = pltpu.get_barrier_semaphore()
    for by in range(1, scens):
        pl.semaphore_signal(entry, inc=1, device_id=(lax.rem(me_s + by, scens), me), device_id_type=MESH)

    @pl.when(has_next)
    def _():
        pl.semaphore_signal(entry, inc=1, device_id=(me_s, me + 1), device_id_type=MESH)

    @pl.when(has_prev)
    def _():
        pl.semaphore_signal(entry, inc=1, device_id=(me_s, me - 1), device_id_type=MESH)

    zero = jnp.zeros(second.shape[1:], F32)
    for ref in recs:
        ref[rows] = zero
    outs[ties] = zero
    own[ties] = zero
    for iteration in range(ITERS):
        got_terms[iteration][slots] = zero.astype(BF16)
    first_t[...] = commit_t[...]

    @pl.when(jnp.logical_not(has_prev))
    def _():
        for iteration in range(ITERS):
            got_terms[iteration][pl.ds(0, slots)] = jnp.zeros((slots,) + second.shape[1:], BF16)

    @pl.when(jnp.logical_not(has_next))
    def _():
        for iteration in range(ITERS):
            got_bar[iteration][...] = jnp.zeros((slots,) + second.shape[1:], BF16)

    pl.semaphore_wait(entry, scens - 1 + has_next.astype(jnp.int32) + has_prev.astype(jnp.int32))

    lanes = lax.broadcasted_iota(jnp.int32, second.shape[1:], 1)
    span = slots // CHUNKS

    def terms_copy(iteration, c):
        return pltpu.make_async_remote_copy(
            src_ref=send_terms.at[pl.ds(c * span, span)],
            dst_ref=got_terms[iteration].at[pl.ds(c * span, span)],
            send_sem=terms_ssem.at[iteration, c],
            recv_sem=terms_rsem.at[iteration, c],
            device_id=(me_s, me + 1),
            device_id_type=MESH,
        )

    def bar_copy(iteration, c):
        return pltpu.make_async_remote_copy(
            src_ref=send_bar.at[pl.ds(c * span, span)],
            dst_ref=got_bar[iteration].at[pl.ds(c * span, span)],
            send_sem=bar_ssem.at[iteration, c],
            recv_sem=bar_rsem.at[iteration, c],
            device_id=(me_s, me - 1),
            device_id_type=MESH,
        )

    def first_copy(iteration, by):
        return pltpu.make_async_remote_copy(
            src_ref=send_first.at[iteration],
            dst_ref=got_first.at[iteration, by],
            send_sem=first_ssem.at[iteration, by],
            recv_sem=first_rsem.at[iteration, by],
            device_id=(lax.rem(me_s + by, scens), me),
            device_id_type=MESH,
        )

    def chain_ties(base, count, news):
        parts_of = [transposed_dot(tie[base + u], news[u].astype(BF16)) for u in range(count)]
        for u in range(count):
            j = base + u
            own[j] = parts_of[u][:BLK] + own[at("prev_own", j)]
            outs[j] = parts_of[u][BLK:] + outs[at("prev_out", j)]

    def start_ties(base, count, carry):
        news = [jnp.where(has_next, mu[base + u], 0.0) for u in range(count)]
        for u in range(count):
            mu[base + u] = news[u]
        chain_ties(base, count, news)
        return carry

    def next_ties(iteration, more):
        def step(base, count, carry):
            news = []
            for u in range(count):
                j = base + u
                stacked = jnp.concatenate([bar[at("right", j)], got_bar[iteration][at("slot_of_tie", j)]], axis=0)
                product = jnp.dot(tie[j], stacked, preferred_element_type=F32)
                news.append(jnp.where(has_next, mu[j] - dual_step * product, 0.0))
            for u in range(count):
                mu[base + u] = news[u]
            if more:
                chain_ties(base, count, news)
            return carry

        loop(ties, step)

    def send_all_terms(iteration):
        def chunk(c, carry):
            def step(base, count, inner):
                blocks_of = [outs[at("last_out", c * span + base + u)] for u in range(count)]
                for u in range(count):
                    send_terms[c * span + base + u] = blocks_of[u].astype(BF16)
                return inner

            loop(span, step)

            @pl.when(has_next)
            def _():
                terms_copy(iteration, c).start()

            return carry

        lax.fori_loop(0, CHUNKS, chunk, 0)

    def chain_rows(base, count, halves, total):
        parts_of = [transposed_dot(coupling[base + u], halves[u]) for u in range(count)]
        for u in range(count):
            r = base + u
            for k in range(KW):
                recs[k][r] = parts_of[u][k * BLK : (k + 1) * BLK] + recs[k][at("prev_rec", k * rows + r)]
            summed = jnp.sum(parts_of[u][KW * BLK :], axis=1, keepdims=True)
            total = total + jnp.where(lanes == at("link", r), summed, 0.0)
        return total

    def start_rows(base, count, total):
        news = [jnp.where(base + u < at("count", 0), lam[base + u], 0.0) for u in range(count)]
        for u in range(count):
            lam[base + u] = news[u]
        return chain_rows(base, count, [new.astype(BF16) for new in news], total)

    def next_rows(more):
        def step(base, count, state):
            total, demand = state
            news = []
            for u in range(count):
                r = base + u
                gathered = [bar[at("pattern", r * KW + k)] for k in range(KW)] + [first_wide[at("link", r)]]
                coupled = jnp.dot(coupling[r], jnp.concatenate(gathered, axis=0), preferred_element_type=F32)
                target = spread(demand, u) + wind[r].astype(F32)
                new = lam[r] + dual_step * (target - coupled)
                news.append(jnp.where(r < at("count", 0), new, 0.0))
            for u in range(count):
                lam[base + u] = news[u]
            if more:
                total = chain_rows(base, count, [new.astype(BF16) for new in news], total)
            return total, pltpu.roll(demand, demand.shape[1] - count, 1)

        return loop(rows, step, (zero, demand_t[...]))[0]

    def send_first_sum(iteration, total):
        send_first[iteration] = (total / scen_total).astype(BF16)
        for by in range(1, scens):
            first_copy(iteration, by).start()

    def move_first(iteration):
        total = send_first[iteration].astype(F32)
        for by in range(1, scens):
            first_copy(iteration, by).wait()
            total = total + got_first[iteration, by].astype(F32)
        now = first_t[...]
        new = jnp.clip(now - first_step * (commit_cost_t[...] - total), 0.0, 1.0)
        first_t[...] = new
        extrapolated = 2.0 * new - now

        def step(base, count, columns):
            for u in range(count):
                first_wide[base + u] = spread(columns, u).astype(BF16)
            return pltpu.roll(columns, columns.shape[1] - count, 1)

        loop(blocks, step, extrapolated)

    def gather_local(base, count, cost):
        moved = []
        for u in range(count):
            b = base + u
            grad = own[at("last_own", b)]
            for k in range(KW):
                grad = grad + recs[k][at("last_rec", k * blocks + b)]
            moved.append(second[b] - primal_step * (spread(cost, u) - grad))
        for u in range(count):
            outs[base + u] = moved[u]
        return pltpu.roll(cost, cost.shape[1] - count, 1)

    def answer_terms(iteration):
        def chunk(c, carry):
            @pl.when(has_prev)
            def _():
                terms_copy(iteration, c).wait_recv()

                def step(base, count, inner):
                    bars = []
                    for u in range(count):
                        d = c * span + base + u
                        b = at("block_of_slot", d)
                        new = jnp.maximum(outs[b] + primal_step * got_terms[iteration][d].astype(F32), 0.0)
                        bars.append((2.0 * new - second[b]).astype(BF16))
                    for u in range(count):
                        send_bar[c * span + base + u] = bars[u]
                    return inner

                loop(span, step)
                bar_copy(iteration, c).start()

            return carry

        lax.fori_loop(0, CHUNKS, chunk, 0)

    def move_second(iteration):
        def step(base, count, carry):
            news = []
            for u in range(count):
                b = base + u
                terms = got_terms[iteration][at("slot_of_block", b)].astype(F32)
                new = jnp.maximum(outs[b] + primal_step * terms, 0.0)
                news.append((new, (2.0 * new - second[b]).astype(BF16)))
            for u in range(count):
                second[base + u], bar[base + u] = news[u]
            return carry

        loop(blocks, step)

    def finish_sends(copy, iteration):
        def chunk(c, carry):
            copy(iteration, c).wait_send()
            return carry

        lax.fori_loop(0, CHUNKS, chunk, 0)

    def finish_receives(copy, iteration):
        def chunk(c, carry):
            copy(iteration, c).wait_recv()
            return carry

        lax.fori_loop(0, CHUNKS, chunk, 0)

    loads[0].wait()
    loads[1].wait()
    loop(ties, start_ties)
    send_all_terms(0)
    loads[2].wait()
    loads[3].wait()
    total = loop(rows, start_rows, zero)
    send_first_sum(0, total)
    loads[4].wait()
    for iteration in range(ITERS):
        more = iteration < ITERS - 1
        loop(blocks, gather_local, cost_t[...])
        answer_terms(iteration)
        move_second(iteration)
        move_first(iteration)
        if iteration == 0:
            loads[5].wait()
        if not more:
            commit_out[...] = first_t[...]
            store_second = pltpu.make_async_copy(second, second_out, store_sems.at[0])
            store_second.start()
        total = next_rows(more)
        if more:
            send_first_sum(iteration + 1, total)
        else:
            store_lam = pltpu.make_async_copy(lam, lam_out, store_sems.at[1])
            store_lam.start()

        @pl.when(has_next)
        def _():
            finish_sends(terms_copy, iteration)
            finish_receives(bar_copy, iteration)

        next_ties(iteration, more)
        if more:
            send_all_terms(iteration + 1)

        @pl.when(has_prev)
        def _():
            finish_sends(bar_copy, iteration)

    store_mu = pltpu.make_async_copy(mu, mu_out, store_sems.at[2])
    store_mu.start()
    store_second.wait()
    store_lam.wait()
    store_mu.wait()


def previous_equal(keys):
    n = keys.shape[-1]
    u = lax.iota(jnp.int32, n)
    same = (keys[..., :, None] == keys[..., None, :]) & (u[None, :] < u[:, None])
    found = jnp.max(jnp.where(same, u[None, :], -1), axis=-1)
    return jnp.where(found < 0, n, found)


def last_equal(keys, wanted):
    n = keys.shape[-1]
    u = lax.iota(jnp.int32, n)
    found = jnp.max(jnp.where(keys[..., None, :] == wanted[:, None], u, -1), axis=-1)
    return jnp.where(found < 0, n, found)


def slot_table(bounds, blocks, slots):
    b = lax.iota(jnp.int32, blocks)
    present = jnp.any(bounds[None, :] == b[:, None], axis=1)
    before = jnp.sum((present[None, :] & (b[None, :] < b[:, None])).astype(jnp.int32), axis=1)
    d = lax.iota(jnp.int32, slots)
    chosen = present[None, :] & (before[None, :] == d[:, None])
    block_of_slot = jnp.sum(jnp.where(chosen, b[None, :], 0), axis=1)
    used = jnp.any(chosen, axis=1)
    return present, before, block_of_slot, used


def body(
    coupling,
    tie_blocks,
    w_pattern,
    link_pattern,
    left_bounds,
    right_bounds,
    block_counts,
    commit_cost,
    dispatch_cost,
    demand,
    wind_error,
    commit_start,
    dispatch_start,
    dual_start,
    tie_start,
):
    parts = lax.axis_size("net")
    scens = lax.axis_size("scen")
    rows, ties, blocks = dual_start.shape[0], tie_start.shape[0], dispatch_start.shape[0]
    block_shape = dispatch_start.shape[1:]
    slots = blocks
    left_next = lax.ppermute(left_bounds, "net", [(i + 1, i) for i in range(parts - 1)])
    b = lax.iota(jnp.int32, blocks)
    keys = w_pattern.T
    present, before, block_of_slot, _ = slot_table(left_bounds, blocks, slots)
    present_next, before_next, block_next, used_next = slot_table(left_next, blocks, slots)
    slot_of_tie = jnp.sum((present_next[None, :] & (b[None, :] < left_next[:, None])).astype(jnp.int32), axis=1)
    last_out = jnp.where(used_next, last_equal(left_next, block_next), ties)
    offsets = layout_of(rows, ties, blocks, slots)
    index = jnp.concatenate(
        [
            block_counts,
            w_pattern.reshape(-1),
            link_pattern,
            previous_equal(keys).reshape(-1),
            last_equal(keys, b).reshape(-1),
            right_bounds,
            previous_equal(right_bounds),
            last_equal(right_bounds, b),
            previous_equal(left_next),
            last_out,
            slot_of_tie,
            jnp.where(present, before, slots),
            block_of_slot,
        ]
    )
    lanes = block_shape[1]

    def turned(value):
        return jnp.pad(value.T, ((0, 0), (0, lanes - value.shape[0])))

    vmem = pl.BlockSpec(memory_space=pltpu.VMEM)
    anywhere = pl.BlockSpec(memory_space=pl.ANY)
    wide = lambda count, kind: pltpu.VMEM((count,) + block_shape, kind)
    sems = pltpu.SemaphoreType.DMA
    commit_t, second, lam, mu = pl.pallas_call(
        functools.partial(kernel, offsets),
        out_shape=(
            jax.ShapeDtypeStruct((BLK, blocks), F32),
            jax.ShapeDtypeStruct(dispatch_start.shape, F32),
            jax.ShapeDtypeStruct(dual_start.shape, F32),
            jax.ShapeDtypeStruct(tie_start.shape, F32),
        ),
        in_specs=[pl.BlockSpec(memory_space=pltpu.SMEM)] + [vmem] * 4 + [anywhere] * 6,
        out_specs=(vmem, anywhere, anywhere, anywhere),
        scratch_shapes=[
            pltpu.VMEM(coupling.shape, BF16),
            pltpu.VMEM(tie_blocks.shape, BF16),
            pltpu.VMEM(wind_error.shape, BF16),
            wide(blocks, F32),
            wide(rows, F32),
            wide(ties, F32),
            wide(rows + 1, F32),
            wide(rows + 1, F32),
            wide(rows + 1, F32),
            wide(rows + 1, F32),
            wide(ties + 1, F32),
            wide(ties + 1, F32),
            wide(slots, BF16),
            wide(slots + 1, BF16),
            wide(slots + 1, BF16),
            wide(slots, BF16),
            wide(slots, BF16),
            wide(slots, BF16),
            wide(blocks, BF16),
            wide(blocks, BF16),
            pltpu.VMEM(block_shape, F32),
            pltpu.VMEM((ITERS,) + block_shape, BF16),
            pltpu.VMEM((ITERS, scens) + block_shape, BF16),
            sems((6,)),
            sems((3,)),
            sems((ITERS, CHUNKS)),
            sems((ITERS, CHUNKS)),
            sems((ITERS, CHUNKS)),
            sems((ITERS, CHUNKS)),
            sems((ITERS, scens)),
            sems((ITERS, scens)),
        ],
        compiler_params=pltpu.CompilerParams(
            collective_id=0, has_side_effects=True, vmem_limit_bytes=62 * 2**20
        ),
        cost_estimate=pl.CostEstimate(flops=32 * 10**8, bytes_accessed=30 * 10**6, transcendentals=0),
    )(
        index,
        turned(dispatch_cost),
        turned(demand),
        turned(commit_cost),
        turned(commit_start),
        coupling,
        tie_blocks,
        wind_error,
        dispatch_start,
        dual_start,
        tie_start,
    )
    return commit_t.T[: commit_start.shape[0]], second, lam, mu


def solution(mesh):
    return jax.shard_map(
        body,
        mesh=mesh,
        in_specs=(
            P("net", None, None),
            P("net", None, None),
            P("net", None),
            P("net"),
            P("net"),
            P("net"),
            P("net"),
            P("net", None),
            P("net", None),
            P("net", None),
            P("net", None, "scen"),
            P("net", None),
            P("net", None, "scen"),
            P("net", None, "scen"),
            P("net", None, "scen"),
        ),
        out_specs=(
            P("net", None),
            P("net", None, "scen"),
            P("net", None, "scen"),
            P("net", None, "scen"),
        ),
        check_vma=False,
    )
```

time: 163 us -> 136 us (0.83)
  waiting for transfers between devices: 41.7 us -> 0.01 us
  Pallas kernels: 78 us -> 112 us
  starting transfers between devices: 19.7 us -> 1.97 us
  other arithmetic: 10.1 us -> 4.48 us
  local copies, waits for them, and re-layouts: 10.7 us -> 15.4 us
    ppermute x10 -> x1, waiting for transfers between devices: 41.7 us -> 0.01 us  [body(): lax.ppermute(left_bounds, 'net', [(i + 1, i) for i in range(parts - 1)])]
    pallas_call x9 -> x1, Pallas kernels: 78 us -> 112 us  [body(): pl.pallas_call(functools.partial(kernel, offsets), out_shape=(jax.ShapeDt...]
    ppermute x10 -> x1, starting transfers between devices: 19.7 us -> 1.97 us  [body(): lax.ppermute(left_bounds, 'net', [(i + 1, i) for i in range(parts - 1)])]
    unnamed x38 -> x9, local copies, waits for them, and re-layouts: 4.78 us -> 12.4 us
    reduce_sum x2 -> x4, other arithmetic: 6.69 us -> 0.55 us  [the longest x1 0.22 us: body(): jnp.sum((present_next[None, :] & (b[None, :] < left_next[:, None])).astyp...]
    broadcast_in_dim x3 -> x0, local copies, waits for them, and re-layouts: 5.78 us -> none  [the longest x2 3.22 us: body(): first_wide = jnp.broadcast_to(first_bar[:, :, None], wide_shape)]
    add x3 -> x0, other arithmetic: 3.3 us -> none  [the longest x1 3.26 us: body(): target = demand[:, :, None] + wind_error.astype(F32)]
    reduce_max x0 -> x4, other arithmetic: none -> 2.9 us  [the longest x3 1.9 us: last_equal(): jnp.max(jnp.where(keys[..., None, :] == wanted[:, None], u, -1), axis=-1)]
  transfers between devices with their start and end apart: 10 -> 1, of which waited for: 9 -> 0; matrix products, arithmetic and copies ran while one was open for 9% -> 5% of each run, Pallas kernels for 20% -> 0%
where the time goes in v1:
time: 136 us; the launch traced here: 135 us
  Pallas kernels  112 us (82%)
  local copies, waits for them, and re-layouts  15.4 us (11%)
  other arithmetic  4.48 us (3%)
  starting transfers between devices  1.97 us (1%)
  between operations  1.38 us (1%)
    pallas_call x1, Pallas kernels, body(): pl.pallas_call(functools.partial(kernel, offsets), out_shape=(jax.ShapeDt...  112 us
    unnamed x9, local copies, waits for them, and re-layouts  12.4 us
  transfers between devices with their start and end apart: 1, of which 0 were waited for; matrix products, arithmetic and copies ran while one was open for 5% of the time, Pallas kernels for 0%

profile of v1, /device:TPU:1, one launch (start us, length us, event | category | flops | bytes accessed | tf_op | source)
XLA Modules:
  0.0 135.0 jit_solution(11994472148880442996)
XLA Ops:
  0.6 2.0 %collective-permute-start = (s32[128]{0:T(128)}, s32[128]{0:T(128)S(1)}, u32[]{:S(2)}, u32[]{:S(2)}) collective-permute-start(s32[128]{0:T(128)} %param.19), channel_id=1, source_target_pairs={{1,0},{2,1},{3,2},{4,3},{5,4},{6,5},{7,6},{9,8},{10,9},{11,10},{12... | collective-permute-start | bytes 1544 | tf_op jit(solution)/shard_map/ppermute | solution.py:462
  2.6 0.8 fusion.8
  3.4 0.1 convert_reduce_fusion
  3.5 0.9 select_reduce_fusion.6
  4.4 0.8 select_reduce_fusion
  5.3 1.0 select_reduce_fusion.1
  6.3 0.1 reduce_max.59
  6.3 0.1 select_reduce_fusion.2
  6.5 0.8 copy.20
  7.9 0.1 reshape.39
  8.0 1.4 %pad.4.demand_t = f32[64,128]{1,0:T(8,128)} pad(f32[64,96]{1,0:T(8,128)} %bitcast.11, f32[]{:T(128)} %constant.5.clone.1), padding=0_0x0_32 | pad | bytes 57348 | tf_op jit(solution)/shard_map/jit(_pad)/pad | solution.py:490
  9.4 0.0 collective-permute-done
  9.4 0.1 fusion.4
  9.5 0.1 convert_reduce_fusion.2
  9.6 0.1 fusion.6
  9.7 0.2 convert_reduce_fusion.1
  10.0 0.2 select_reduce_fusion.3
  10.2 1.4 %concatenate.3.index = s32[2401]{0:T(1024)} concatenate(s32[1]{0:T(128)S(6)} %copy.25, s32[384]{0:T(512)S(1)} %reshape.39, s32[96]{0:T(128)} %param.18, s32[384]{0:T(512)S(1)} %compare_select_fusion.1, s32[512]{0:T(512)S(1)} %compare_select_fusion, s32[128]{0:T(128)} %param.20, s32[128]{0:T(128)S(1)} %get-tuple-element.18, s32[128]{0:T(128)S(1)} %get-tuple-element.17, ...), dimensions={0} | concatenate | bytes 19208 | tf_op jit(solution)/shard_map/concatenate | solution.py:470
  11.5 111.8 %shard_map.174 = (f32[64,128]{1,0:T(8,128)}, f32[128,64,128]{2,1,0:T(8,128)}, f32[96,64,128]{2,1,0:T(8,128)}, f32[128,64,128]{2,1,0:T(8,128)}) custom-call(s32[2401]{0:T(1024)} %concatenate.3.index, f32[64,128]{1,0:T(8,128)} %bitcast.8, f32[64,128]{1,0:T(8,128)} %pad.4.demand_t, f32[64,128]{1,0:T(8,128)} %bitcast.9, f32[64,128]{1,0:T(8,128)} %bitcast.10, ...), custom_call_target="tpu_custom_call" | custom-call | flops 3200000000 | bytes 30000000 | tf_op jit(solution)/shard_map/pallas_call | solution.py:496
  123.3 1.4 %copy.26 = f32[128,64]{0,1:T(8,128)} copy(f32[128,64]{0,1:T(8,128)} %bitcast.12) | data formatting | bytes 65536
  124.7 0.0 copy-start.1
  124.7 4.9 %copy.27 = f32[128,64,128]{2,1,0:T(8,128)} copy(f32[128,64,128]{2,1,0:T(8,128)} %get-tuple-element.26) | data formatting | bytes 8388608
  129.7 0.0 copy-done.1
  129.7 0.0 copy-start
  129.7 1.7 %copy.28 = f32[96,64,128]{2,1,0:T(8,128)} copy(f32[96,64,128]{2,1,0:T(8,128)S(1)} %copy-done.1) | data formatting | bytes 6291456
  131.3 1.7 %copy-done = f32[128,64,128]{2,1,0:T(8,128)S(1)} copy-done((f32[128,64,128]{2,1,0:T(8,128)S(1)}, f32[128,64,128]{2,1,0:T(8,128)}, u32[]{:S(2)}) %copy-start) | copy-done | bytes 4194328
  133.0 2.0 %copy.29 = f32[128,64,128]{2,1,0:T(8,128)} copy(f32[128,64,128]{2,1,0:T(8,128)S(1)} %copy-done) | data formatting | bytes 8388608
  (6 shorter events, 0.0 us)
Async XLA Ops:
  0.6 8.8 %collective-permute-start = (s32[128]{0:T(128)}, s32[128]{0:T(128)S(1)}, u32[]{:S(2)}, u32[]{:S(2)}) collective-permute-start(s32[128]{0:T(128)} %param.19), channel_id=1, source_target_pairs={{1,0},{2,1},{3,2},{4,3},{5,4},{6,5},{7,6},{9,8},{10,9},{11,10},{12... | collective-permute-start | bytes 1544 | tf_op jit(solution)/shard_map/ppermute | solution.py:462
  124.7 4.9 %copy-start.1 = (f32[96,64,128]{2,1,0:T(8,128)S(1)}, f32[96,64,128]{2,1,0:T(8,128)}, u32[]{:S(2)}) copy-start(f32[96,64,128]{2,1,0:T(8,128)} %get-tuple-element.27) | copy-start | bytes 9437188
  129.7 3.3 %copy-start = (f32[128,64,128]{2,1,0:T(8,128)S(1)}, f32[128,64,128]{2,1,0:T(8,128)}, u32[]{:S(2)}) copy-start(f32[128,64,128]{2,1,0:T(8,128)} %get-tuple-element.28) | copy-start | bytes 12582916

commit v2 on v1

--- a/solution.py
+++ b/solution.py
@@ -35,31 +35,127 @@
     return lax.fori_loop(0, count // unroll, lambda c, state: step(c * unroll, unroll, state), carry)
 
 
-def layout_of(rows, ties, blocks, slots):
-    sizes = dict(
-        count=1,
-        pattern=rows * KW,
-        link=rows,
-        prev_rec=KW * rows,
-        last_rec=KW * blocks,
-        right=ties,
-        prev_own=ties,
-        last_own=blocks,
-        prev_out=ties,
-        last_out=slots,
-        slot_of_tie=ties,
-        slot_of_block=blocks,
-        block_of_slot=slots,
-    )
-    offsets, at = {}, 0
-    for name, size in sizes.items():
-        offsets[name] = at
-        at += size
-    return offsets
+TABLE = dict(
+    pattern=0,
+    link=4,
+    prev_rec=5,
+    last_rec=9,
+    right=13,
+    prev_own=14,
+    last_own=15,
+    prev_out=16,
+    last_out=17,
+    slot_of_tie=18,
+    slot_of_block=19,
+    block_of_slot=20,
+    most=21,
+    count=22,
+)
+TABLE_ROWS = 24
+
+
+def prepare(slots_few, left, right, pattern, link, count, table, most, message, padded, inbox, send_sems, recv_sems):
+    me_s, me = lax.axis_index("scen"), lax.axis_index("net")
+    parts = lax.axis_size("net")
+    lanes = table.shape[1]
+    blocks = lanes
+
+    entry = pltpu.get_barrier_semaphore()
+    for by in range(1, parts):
+        pl.semaphore_signal(entry, inc=1, device_id=(me_s, lax.rem(me + by, parts)), device_id_type=MESH)
+
+    down = lax.broadcasted_iota(jnp.int32, (lanes, lanes), 0)
+    along = lax.broadcasted_iota(jnp.int32, (lanes, lanes), 1)
+
+    def both(row):
+        spread_row = jnp.broadcast_to(row, (lanes, lanes)).astype(F32)
+        return spread_row, spread_row.T
+
+    def most_of(mask, values):
+        return jnp.max(jnp.where(mask, values.astype(F32), -1.0), axis=0, keepdims=True)
+
+    def or_else(found, other):
+        return jnp.where(found < 0.0, jnp.float32(other), found).astype(jnp.int32)
+
+    def chain(row, n):
+        at_lane, at_row = both(row)
+        previous = most_of((at_lane == at_row) & (down < along) & (down < n), down)
+        last = most_of((at_row == along.astype(F32)) & (down < n), down)
+        return previous, last
+
+    def slots_of(row):
+        at_lane, at_row = both(row)
+        hit = at_row == along.astype(F32)
+        present = jnp.max(jnp.where(hit, 1.0, 0.0), axis=0, keepdims=True)
+        present_wide = jnp.broadcast_to(present, (lanes, lanes))
+        present_down = present_wide.T
+        before = jnp.sum(jnp.where(down < along, present_down, 0.0), axis=0, keepdims=True)
+        _, before_down = both(before)
+        chosen = (present_down > 0.0) & (before_down == along.astype(F32))
+        block_of_slot = most_of(chosen, down)
+        return present, before, block_of_slot, jnp.sum(present, axis=1, keepdims=True)
+
+    present, before, block_of_slot, count_of = slots_of(left[...])
+    message[...] = jnp.zeros(message.shape, jnp.int32)
+    message[0:1] = left[...]
+    counted = jnp.broadcast_to(count_of, (1, lanes)).astype(jnp.int32)
+    message[1:2] = jnp.where(me > 0, counted, 0)
+    pl.semaphore_wait(entry, parts - 1)
+
+    def copy(by):
+        return pltpu.make_async_remote_copy(
+            src_ref=message,
+            dst_ref=inbox.at[by],
+            send_sem=send_sems.at[by],
+            recv_sem=recv_sems.at[by],
+            device_id=(me_s, lax.rem(me + by, parts)),
+            device_id_type=MESH,
+        )
+
+    for by in range(1, parts):
+        copy(by).start()
+
+    rows, ties = pattern.shape[1], right.shape[1]
+    table[...] = jnp.zeros(table.shape, jnp.int32)
+    sentinel = jnp.zeros((1, lanes), jnp.int32) + lanes
+    for k in range(KW):
+        padded[...] = sentinel
+        padded[:, 0:rows] = pattern[k : k + 1]
+        row = padded[...]
+        table[TABLE["pattern"] + k : TABLE["pattern"] + k + 1] = row
+        previous, last = chain(row, rows)
+        table[TABLE["prev_rec"] + k : TABLE["prev_rec"] + k + 1] = or_else(previous, rows)
+        table[TABLE["last_rec"] + k : TABLE["last_rec"] + k + 1] = or_else(last, rows)
+    table[TABLE["link"] : TABLE["link"] + 1, 0:rows] = link[...]
+    previous, last = chain(right[...], ties)
+    table[TABLE["right"] : TABLE["right"] + 1] = right[...]
+    table[TABLE["prev_own"] : TABLE["prev_own"] + 1] = or_else(previous, ties)
+    table[TABLE["last_own"] : TABLE["last_own"] + 1] = or_else(last, ties)
+    table[TABLE["slot_of_block"] : TABLE["slot_of_block"] + 1] = jnp.where(present > 0.0, before + 1.0, 0.0).astype(jnp.int32)
+    table[TABLE["block_of_slot"] : TABLE["block_of_slot"] + 1] = or_else(block_of_slot, 0)
+    table[TABLE["count"] : TABLE["count"] + 1] = jnp.zeros((1, lanes), jnp.int32) + count[0]
+
+    highest = message[1:2]
+    for by in range(1, parts):
+        copy(by).wait()
+        highest = jnp.maximum(highest, inbox[by, 1:2])
+    most[...] = jnp.where(highest > slots_few, 1, 0)
+    left_next = inbox[parts - 1, 0:1]
+    previous, last = chain(left_next, ties)
+    present, before, block_of_slot, _ = slots_of(left_next)
+    at_lane, at_row = both(left_next)
+    _, last_down = both(last)
+    _, before_down = both(before)
+    slot_of_tie = most_of(at_lane == down.astype(F32), before_down)
+    _, block_down = both(block_of_slot)
+    block_lane, _ = both(block_of_slot)
+    last_out = most_of(block_lane == down.astype(F32), last_down)
+    table[TABLE["prev_out"] : TABLE["prev_out"] + 1] = or_else(previous, ties)
+    table[TABLE["last_out"] : TABLE["last_out"] + 1] = or_else(last_out, ties)
+    table[TABLE["slot_of_tie"] : TABLE["slot_of_tie"] + 1] = slot_of_tie.astype(jnp.int32)
 
 
 def kernel(
-    offsets,
     index,
     cost_t,
     demand_t,
@@ -96,6 +192,7 @@
     bar,
     first_wide,
     first_t,
+    demand_wide,
     send_first,
     got_first,
     load_sems,
@@ -116,8 +213,8 @@
     scen_total = lam.shape[2] * scens
     has_next, has_prev = me < parts - 1, me > 0
 
-    def at(name, i):
-        return index[offsets[name] + i]
+    def at(name, i, k=0):
+        return index[TABLE[name] + k, i]
 
     loads = [
         pltpu.make_async_copy(src, dst, load_sems.at[i])
@@ -146,13 +243,14 @@
     outs[ties] = zero
     own[ties] = zero
     for iteration in range(ITERS):
-        got_terms[iteration][slots] = zero.astype(BF16)
+        got_terms[iteration][0] = zero.astype(BF16)
     first_t[...] = commit_t[...]
+    demand_wide[:, 0:rows] = demand_t[...]
 
     @pl.when(jnp.logical_not(has_prev))
     def _():
         for iteration in range(ITERS):
-            got_terms[iteration][pl.ds(0, slots)] = jnp.zeros((slots,) + second.shape[1:], BF16)
+            got_terms[iteration][pl.ds(1, slots)] = jnp.zeros((slots,) + second.shape[1:], BF16)
 
     @pl.when(jnp.logical_not(has_next))
     def _():
@@ -167,7 +265,7 @@
     def terms_copy(iteration, c):
         return pltpu.make_async_remote_copy(
             src_ref=send_terms.at[pl.ds(c * span, span)],
-            dst_ref=got_terms[iteration].at[pl.ds(c * span, span)],
+            dst_ref=got_terms[iteration].at[pl.ds(1 + c * span, span)],
             send_sem=terms_ssem.at[iteration, c],
             recv_sem=terms_rsem.at[iteration, c],
             device_id=(me_s, me + 1),
@@ -247,7 +345,7 @@
         for u in range(count):
             r = base + u
             for k in range(KW):
-                recs[k][r] = parts_of[u][k * BLK : (k + 1) * BLK] + recs[k][at("prev_rec", k * rows + r)]
+                recs[k][r] = parts_of[u][k * BLK : (k + 1) * BLK] + recs[k][at("prev_rec", r, k)]
             summed = jnp.sum(parts_of[u][KW * BLK :], axis=1, keepdims=True)
             total = total + jnp.where(lanes == at("link", r), summed, 0.0)
         return total
@@ -264,7 +362,7 @@
             news = []
             for u in range(count):
                 r = base + u
-                gathered = [bar[at("pattern", r * KW + k)] for k in range(KW)] + [first_wide[at("link", r)]]
+                gathered = [bar[at("pattern", r, k)] for k in range(KW)] + [first_wide[at("link", r)]]
                 coupled = jnp.dot(coupling[r], jnp.concatenate(gathered, axis=0), preferred_element_type=F32)
                 target = spread(demand, u) + wind[r].astype(F32)
                 new = lam[r] + dual_step * (target - coupled)
@@ -275,7 +373,7 @@
                 total = chain_rows(base, count, [new.astype(BF16) for new in news], total)
             return total, pltpu.roll(demand, demand.shape[1] - count, 1)
 
-        return loop(rows, step, (zero, demand_t[...]))[0]
+        return loop(rows, step, (zero, demand_wide[...]))[0]
 
     def send_first_sum(iteration, total):
         send_first[iteration] = (total / scen_total).astype(BF16)
@@ -305,7 +403,7 @@
             b = base + u
             grad = own[at("last_own", b)]
             for k in range(KW):
-                grad = grad + recs[k][at("last_rec", k * blocks + b)]
+                grad = grad + recs[k][at("last_rec", b, k)]
             moved.append(second[b] - primal_step * (spread(cost, u) - grad))
         for u in range(count):
             outs[base + u] = moved[u]
@@ -322,7 +420,7 @@
                     for u in range(count):
                         d = c * span + base + u
                         b = at("block_of_slot", d)
-                        new = jnp.maximum(outs[b] + primal_step * got_terms[iteration][d].astype(F32), 0.0)
+                        new = jnp.maximum(outs[b] + primal_step * got_terms[iteration][1 + d].astype(F32), 0.0)
                         bars.append((2.0 * new - second[b]).astype(BF16))
                     for u in range(count):
                         send_bar[c * span + base + u] = bars[u]
@@ -411,32 +509,6 @@
     store_mu.wait()
 
 
-def previous_equal(keys):
-    n = keys.shape[-1]
-    u = lax.iota(jnp.int32, n)
-    same = (keys[..., :, None] == keys[..., None, :]) & (u[None, :] < u[:, None])
-    found = jnp.max(jnp.where(same, u[None, :], -1), axis=-1)
-    return jnp.where(found < 0, n, found)
-
-
-def last_equal(keys, wanted):
-    n = keys.shape[-1]
-    u = lax.iota(jnp.int32, n)
-    found = jnp.max(jnp.where(keys[..., None, :] == wanted[:, None], u, -1), axis=-1)
-    return jnp.where(found < 0, n, found)
-
-
-def slot_table(bounds, blocks, slots):
-    b = lax.iota(jnp.int32, blocks)
-    present = jnp.any(bounds[None, :] == b[:, None], axis=1)
-    before = jnp.sum((present[None, :] & (b[None, :] < b[:, None])).astype(jnp.int32), axis=1)
-    d = lax.iota(jnp.int32, slots)
-    chosen = present[None, :] & (before[None, :] == d[:, None])
-    block_of_slot = jnp.sum(jnp.where(chosen, b[None, :], 0), axis=1)
-    used = jnp.any(chosen, axis=1)
-    return present, before, block_of_slot, used
-
-
 def body(
     coupling,
     tie_blocks,
@@ -454,98 +526,91 @@
     dual_start,
     tie_start,
 ):
-    parts = lax.axis_size("net")
-    scens = lax.axis_size("scen")
-    rows, ties, blocks = dual_start.shape[0], tie_start.shape[0], dispatch_start.shape[0]
+    parts, scens = lax.axis_size("net"), lax.axis_size("scen")
+    blocks = dispatch_start.shape[0]
     block_shape = dispatch_start.shape[1:]
-    slots = blocks
-    left_next = lax.ppermute(left_bounds, "net", [(i + 1, i) for i in range(parts - 1)])
-    b = lax.iota(jnp.int32, blocks)
-    keys = w_pattern.T
-    present, before, block_of_slot, _ = slot_table(left_bounds, blocks, slots)
-    present_next, before_next, block_next, used_next = slot_table(left_next, blocks, slots)
-    slot_of_tie = jnp.sum((present_next[None, :] & (b[None, :] < left_next[:, None])).astype(jnp.int32), axis=1)
-    last_out = jnp.where(used_next, last_equal(left_next, block_next), ties)
-    offsets = layout_of(rows, ties, blocks, slots)
-    index = jnp.concatenate(
-        [
-            block_counts,
-            w_pattern.reshape(-1),
-            link_pattern,
-            previous_equal(keys).reshape(-1),
-            last_equal(keys, b).reshape(-1),
-            right_bounds,
-            previous_equal(right_bounds),
-            last_equal(right_bounds, b),
-            previous_equal(left_next),
-            last_out,
-            slot_of_tie,
-            jnp.where(present, before, slots),
-            block_of_slot,
-        ]
-    )
-    lanes = block_shape[1]
-
-    def turned(value):
-        return jnp.pad(value.T, ((0, 0), (0, lanes - value.shape[0])))
-
+    few = blocks * 3 // 4
     vmem = pl.BlockSpec(memory_space=pltpu.VMEM)
+    smem = pl.BlockSpec(memory_space=pltpu.SMEM)
     anywhere = pl.BlockSpec(memory_space=pl.ANY)
-    wide = lambda count, kind: pltpu.VMEM((count,) + block_shape, kind)
     sems = pltpu.SemaphoreType.DMA
-    commit_t, second, lam, mu = pl.pallas_call(
-        functools.partial(kernel, offsets),
+    table, most = pl.pallas_call(
+        functools.partial(prepare, few),
         out_shape=(
-            jax.ShapeDtypeStruct((BLK, blocks), F32),
-            jax.ShapeDtypeStruct(dispatch_start.shape, F32),
-            jax.ShapeDtypeStruct(dual_start.shape, F32),
-            jax.ShapeDtypeStruct(tie_start.shape, F32),
+            jax.ShapeDtypeStruct((TABLE_ROWS, blocks), jnp.int32),
+            jax.ShapeDtypeStruct((1, blocks), jnp.int32),
         ),
-        in_specs=[pl.BlockSpec(memory_space=pltpu.SMEM)] + [vmem] * 4 + [anywhere] * 6,
-        out_specs=(vmem, anywhere, anywhere, anywhere),
+        in_specs=[vmem] * 4 + [smem],
+        out_specs=(vmem, vmem),
         scratch_shapes=[
-            pltpu.VMEM(coupling.shape, BF16),
-            pltpu.VMEM(tie_blocks.shape, BF16),
-            pltpu.VMEM(wind_error.shape, BF16),
-            wide(blocks, F32),
-            wide(rows, F32),
-            wide(ties, F32),
-            wide(rows + 1, F32),
-            wide(rows + 1, F32),
-            wide(rows + 1, F32),
-            wide(rows + 1, F32),
-            wide(ties + 1, F32),
-            wide(ties + 1, F32),
-            wide(slots, BF16),
-            wide(slots + 1, BF16),
-            wide(slots + 1, BF16),
-            wide(slots, BF16),
-            wide(slots, BF16),
-            wide(slots, BF16),
-            wide(blocks, BF16),
-            wide(blocks, BF16),
-            pltpu.VMEM(block_shape, F32),
-            pltpu.VMEM((ITERS,) + block_shape, BF16),
-            pltpu.VMEM((ITERS, scens) + block_shape, BF16),
-            sems((6,)),
-            sems((3,)),
-            sems((ITERS, CHUNKS)),
-            sems((ITERS, CHUNKS)),
-            sems((ITERS, CHUNKS)),
-            sems((ITERS, CHUNKS)),
-            sems((ITERS, scens)),
-            sems((ITERS, scens)),
+            pltpu.VMEM((8, blocks), jnp.int32),
+            pltpu.VMEM((1, blocks), jnp.int32),
+            pltpu.VMEM((parts, 8, blocks), jnp.int32),
+            sems((parts,)),
+            sems((parts,)),
         ],
-        compiler_params=pltpu.CompilerParams(
-            collective_id=0, has_side_effects=True, vmem_limit_bytes=62 * 2**20
-        ),
-        cost_estimate=pl.CostEstimate(flops=32 * 10**8, bytes_accessed=30 * 10**6, transcendentals=0),
-    )(
-        index,
-        turned(dispatch_cost),
-        turned(demand),
-        turned(commit_cost),
-        turned(commit_start),
+        compiler_params=pltpu.CompilerParams(collective_id=0, has_side_effects=True),
+    )(left_bounds[None], right_bounds[None], w_pattern.T, link_pattern[None], block_counts)
+
+    def call(slots, collective_id, operands):
+        wide = lambda count, kind: pltpu.VMEM((count,) + block_shape, kind)
+        rows, ties = dual_start.shape[0], tie_start.shape[0]
+        return pl.pallas_call(
+            kernel,
+            out_shape=(
+                jax.ShapeDtypeStruct((BLK, blocks), F32),
+                jax.ShapeDtypeStruct(dispatch_start.shape, F32),
+                jax.ShapeDtypeStruct(dual_start.shape, F32),
+                jax.ShapeDtypeStruct(tie_start.shape, F32),
+            ),
+            in_specs=[smem] + [vmem] * 4 + [anywhere] * 6,
+            out_specs=(vmem, anywhere, anywhere, anywhere),
+            scratch_shapes=[
+                pltpu.VMEM(coupling.shape, BF16),
+                pltpu.VMEM(tie_blocks.shape, BF16),
+                pltpu.VMEM(wind_error.shape, BF16),
+                wide(blocks, F32),
+                wide(rows, F32),
+                wide(ties, F32),
+                wide(rows + 1, F32),
+                wide(rows + 1, F32),
+                wide(rows + 1, F32),
+                wide(rows + 1, F32),
+                wide(ties + 1, F32),
+                wide(ties + 1, F32),
+                wide(slots, BF16),
+                wide(slots + 1, BF16),
+                wide(slots + 1, BF16),
+                wide(slots, BF16),
+                wide(slots, BF16),
+                wide(slots, BF16),
+                wide(blocks, BF16),
+                wide(blocks, BF16),
+                pltpu.VMEM(block_shape, F32),
+                pltpu.VMEM(block_shape, F32),
+                pltpu.VMEM((ITERS,) + block_shape, BF16),
+                pltpu.VMEM((ITERS, scens) + block_shape, BF16),
+                sems((6,)),
+                sems((3,)),
+                sems((ITERS, CHUNKS)),
+                sems((ITERS, CHUNKS)),
+                sems((ITERS, CHUNKS)),
+                sems((ITERS, CHUNKS)),
+                sems((ITERS, scens)),
+                sems((ITERS, scens)),
+            ],
+            compiler_params=pltpu.CompilerParams(
+                collective_id=collective_id, has_side_effects=True, vmem_limit_bytes=62 * 2**20
+            ),
+            cost_estimate=pl.CostEstimate(flops=32 * 10**8, bytes_accessed=30 * 10**6, transcendentals=0),
+        )(*operands)
+
+    operands = (
+        table,
+        dispatch_cost.T,
+        demand.T,
+        commit_cost.T,
+        commit_start.T,
         coupling,
         tie_blocks,
         wind_error,
@@ -553,7 +618,13 @@
         dual_start,
         tie_start,
     )
-    return commit_t.T[: commit_start.shape[0]], second, lam, mu
+    commit_t, second, lam, mu = lax.cond(
+        most[0, 0] > 0,
+        lambda *given: call(blocks, 1, given),
+        lambda *given: call(few, 2, given),
+        *operands,
+    )
+    return commit_t.T, second, lam, mu
 
 
 def solution(mesh):

time: 136 us -> 108 us (0.79)
  Pallas kernels: 112 us -> 94.4 us
  local copies, waits for them, and re-layouts: 15.4 us -> 10.9 us
  other arithmetic: 4.48 us -> 0 us
  starting transfers between devices: 1.97 us -> 0 us
    pallas_call x1 -> x2, Pallas kernels: 112 us -> 94.4 us  [the longest x1 87 us: call(): pl.pallas_call(kernel, out_shape=(jax.ShapeDtypeStruct((BLK, blocks), F32...]
    reduce_max x4 -> x0, other arithmetic: 2.9 us -> none  [the longest x3 1.9 us: last_equal(): jnp.max(jnp.where(keys[..., None, :] == wanted[:, None], u, -1), axis=-1)]
    ppermute x1 -> x0, starting transfers between devices: 1.97 us -> none  [body(): lax.ppermute(left_bounds, 'net', [(i + 1, i) for i in range(parts - 1)])]
    unnamed x9 -> x8, local copies, waits for them, and re-layouts: 12.4 us -> 10.9 us
    pad x1 -> x0, local copies, waits for them, and re-layouts: 1.38 us -> none  [turned(): return jnp.pad(value.T, ((0, 0), (0, lanes - value.shape[0])))]
  transfers between devices with their start and end apart: 1 -> 0, of which waited for: 0 -> 0; matrix products, arithmetic and copies ran while one was open for 5% -> 0% of each run, Pallas kernels for 0% -> 0%
where the time goes in v2:
time: 108 us; the launch traced here: 107 us
  Pallas kernels  94.4 us (87%)
  local copies, waits for them, and re-layouts  10.9 us (10%)
  between operations  1.99 us (2%)
    pallas_call x1, Pallas kernels, call(): pl.pallas_call(kernel, out_shape=(jax.ShapeDtypeStruct((BLK, blocks), F32...  87 us
    unnamed x8, local copies, waits for them, and re-layouts  10.9 us
    pallas_call x1, Pallas kernels, body(): pl.pallas_call(functools.partial(prepare, few), out_shape=(jax.ShapeDtype...  7.45 us

profile of v2, /device:TPU:1, one launch (start us, length us, event | category | flops | bytes accessed | tf_op | source)
XLA Modules:
  0.0 107.3 jit_solution(7149708223903818777)
XLA Ops:
  1.3 7.5 %shard_map.174 = (s32[24,128]{1,0:T(8,128)S(1)}, s32[1,128]{1,0:T(1,128)}) custom-call(s32[1,128]{1,0:T(1,128)} %bitcast.21, s32[1,128]{1,0:T(1,128)} %bitcast.22, s32[4,96]{1,0:T(4,128)} %bitcast.20, s32[1,96]{1,0:T(1,128)} %bitcast.23, s32[1]{0:T(128)S(6)} %copy.31.count), custom_call_target="tpu_custom_call" | custom-call | tf_op jit(solution)/shard_map/pallas_call | solution.py:537
  9.4 87.0 %conditional.1 = ((f32[64,128]{1,0:T(8,128)S(1)}, f32[128,64,128]{2,1,0:T(8,128)}, f32[96,64,128]{2,1,0:T(8,128)}, f32[128,64,128]{2,1,0:T(8,128)})) conditional(s32[]{:T(128)} %bitcast.4, (s32[24,128]{1,0:T(8,128)S(1)}, f32[64,128]{1,0:T(8,128)}, f32[64,96]{1,0:T(8,128)}, f32[64,128]{1,0:T(8,128)}, f32[64,128]{1,0:T(8,128)}, ...), branch_computations={%region_0.0_spmd, %region_1.0_spmd} | conditional | flops 3200000000 | bytes 30000008 | solution.py:621
  9.4 87.0 %branch_0_fun.1 = (f32[64,128]{1,0:T(8,128)S(1)}, f32[128,64,128]{2,1,0:T(8,128)}, f32[96,64,128]{2,1,0:T(8,128)}, f32[128,64,128]{2,1,0:T(8,128)}) custom-call(s32[24,128]{1,0:T(8,128)S(1)} %get-tuple-element.44.index, f32[64,128]{1,0:T(8,128)} %get-tuple-element.45.cost_t, f32[64,96]{1,0:T(8,128)} %get-tuple-element.46.demand_t, ...), custom_call_target="tpu_custom_call" | custom-call | flops 3200000000 | bytes 30000000 | tf_op jit(solution)/shard_map/cond/branch_0_fun/pallas_call | solution.py:558
  96.4 0.6 copy.32
  97.1 0.0 copy-start.1
  97.1 4.9 %copy.33 = f32[128,64,128]{2,1,0:T(8,128)} copy(f32[128,64,128]{2,1,0:T(8,128)} %get-tuple-element.95) | data formatting | bytes 8388608
  102.0 0.0 copy-done.1
  102.0 0.0 copy-start
  102.0 1.7 %copy.34 = f32[96,64,128]{2,1,0:T(8,128)} copy(f32[96,64,128]{2,1,0:T(8,128)S(1)} %copy-done.1) | data formatting | bytes 6291456
  103.7 1.7 %copy-done = f32[128,64,128]{2,1,0:T(8,128)S(1)} copy-done((f32[128,64,128]{2,1,0:T(8,128)S(1)}, f32[128,64,128]{2,1,0:T(8,128)}, u32[]{:S(2)}) %copy-start) | copy-done | bytes 4194328
  105.3 2.0 %copy.35 = f32[128,64,128]{2,1,0:T(8,128)} copy(f32[128,64,128]{2,1,0:T(8,128)S(1)} %copy-done) | data formatting | bytes 8388608
Async XLA Ops:
  97.1 4.9 %copy-start.1 = (f32[96,64,128]{2,1,0:T(8,128)S(1)}, f32[96,64,128]{2,1,0:T(8,128)}, u32[]{:S(2)}) copy-start(f32[96,64,128]{2,1,0:T(8,128)} %get-tuple-element.96) | copy-start | bytes 9437188
  102.0 3.3 %copy-start = (f32[128,64,128]{2,1,0:T(8,128)S(1)}, f32[128,64,128]{2,1,0:T(8,128)}, u32[]{:S(2)}) copy-start(f32[128,64,128]{2,1,0:T(8,128)} %get-tuple-element.97) | copy-start | bytes 12582916

commit v3 on v2

--- a/solution.py
+++ b/solution.py
@@ -12,6 +12,7 @@
 ITERS = 2
 CHUNKS = 8
 UNROLL = 16
+RELAYED = 8
 
 primal_step = 0.4
 first_step = 1.0
@@ -189,6 +190,8 @@
     send_bar,
     got_bar0,
     got_bar1,
+    relay0,
+    relay1,
     bar,
     first_wide,
     first_t,
@@ -201,17 +204,22 @@
     terms_rsem,
     bar_ssem,
     bar_rsem,
+    relay_ssem,
+    relay_rsem,
     first_ssem,
     first_rsem,
 ):
     recs = (rec0, rec1, rec2, rec3)
-    got_terms, got_bar = (got_terms0, got_terms1), (got_bar0, got_bar1)
+    got_terms, got_bar, relay = (got_terms0, got_terms1), (got_bar0, got_bar1), (relay0, relay1)
     me_s, me = lax.axis_index("scen"), lax.axis_index("net")
     scens, parts = lax.axis_size("scen"), lax.axis_size("net")
     rows, ties, blocks = lam.shape[0], mu.shape[0], second.shape[0]
     slots = send_terms.shape[0]
     scen_total = lam.shape[2] * scens
     has_next, has_prev = me < parts - 1, me > 0
+    relayed = parts == RELAYED
+    low, high = parts // 2 - 1, parts // 2
+    is_low, is_high, is_first, is_last = me == low, me == high, me == 0, me == parts - 1
 
     def at(name, i, k=0):
         return index[TABLE[name] + k, i]
@@ -236,6 +244,17 @@
     @pl.when(has_prev)
     def _():
         pl.semaphore_signal(entry, inc=1, device_id=(me_s, me - 1), device_id_type=MESH)
+
+    greeted = scens - 1 + has_next.astype(jnp.int32) + has_prev.astype(jnp.int32)
+    if relayed:
+        for mine, others in ((0, (low, high)), (parts - 1, (low, high)), (low, (0, parts - 1)), (high, (0, parts - 1))):
+
+            @pl.when(me == mine)
+            def _(others=others):
+                for other in others:
+                    pl.semaphore_signal(entry, inc=1, device_id=(me_s, jnp.int32(other)), device_id_type=MESH)
+
+            greeted = greeted + 2 * (me == mine).astype(jnp.int32)
 
     zero = jnp.zeros(second.shape[1:], F32)
     for ref in recs:
@@ -257,7 +276,7 @@
         for iteration in range(ITERS):
             got_bar[iteration][...] = jnp.zeros((slots,) + second.shape[1:], BF16)
 
-    pl.semaphore_wait(entry, scens - 1 + has_next.astype(jnp.int32) + has_prev.astype(jnp.int32))
+    pl.semaphore_wait(entry, greeted)
 
     lanes = lax.broadcasted_iota(jnp.int32, second.shape[1:], 1)
     span = slots // CHUNKS
@@ -281,6 +300,67 @@
             device_id=(me_s, me - 1),
             device_id_type=MESH,
         )
+
+    def to_relay(iteration, c, source, send_sem, device):
+        return pltpu.make_async_remote_copy(
+            src_ref=source.at[pl.ds(c * span, span)],
+            dst_ref=relay[iteration].at[pl.ds(c // 2 * span, span)],
+            send_sem=send_sem.at[iteration, c],
+            recv_sem=relay_rsem.at[iteration, c],
+            device_id=(me_s, jnp.int32(device)),
+            device_id_type=MESH,
+        )
+
+    def from_relay(iteration, c, target, shift, recv_sem, device):
+        return pltpu.make_async_remote_copy(
+            src_ref=relay[iteration].at[pl.ds(c // 2 * span, span)],
+            dst_ref=target[iteration].at[pl.ds(shift + c * span, span)],
+            send_sem=relay_ssem.at[iteration, c],
+            recv_sem=recv_sem.at[iteration, c],
+            device_id=(me_s, jnp.int32(device)),
+            device_id_type=MESH,
+        )
+
+    def terms_relay(iteration, c):
+        return to_relay(iteration, c, send_terms, terms_ssem, parts - 1)
+
+    def terms_onward(iteration, c):
+        return from_relay(iteration, c, got_terms, 1, terms_rsem, high)
+
+    def bar_relay(iteration, c):
+        return to_relay(iteration, c, send_bar, bar_ssem, 0)
+
+    def bar_onward(iteration, c):
+        return from_relay(iteration, c, got_bar, 0, bar_rsem, low)
+
+    def start_split(iteration, c, sender, direct, relay_of):
+        if not relayed:
+            direct(iteration, c).start()
+            return
+        by_relay = sender & (lax.rem(c, 2) == 1)
+
+        @pl.when(by_relay)
+        def _():
+            relay_of(iteration, c).start()
+
+        @pl.when(jnp.logical_not(by_relay))
+        def _():
+            direct(iteration, c).start()
+
+    def pass_on(iteration, arriving, onward):
+        def step(h, carry):
+            arriving(iteration, 2 * h + 1).wait_recv()
+            onward(iteration, 2 * h + 1).start()
+            return carry
+
+        lax.fori_loop(0, CHUNKS // 2, step, 0)
+
+    def finish_onward(iteration, onward):
+        def step(h, carry):
+            onward(iteration, 2 * h + 1).wait_send()
+            return carry
+
+        lax.fori_loop(0, CHUNKS // 2, step, 0)
 
     def first_copy(iteration, by):
         return pltpu.make_async_remote_copy(
@@ -334,11 +414,16 @@
 
             @pl.when(has_next)
             def _():
-                terms_copy(iteration, c).start()
+                start_split(iteration, c, is_low, terms_copy, terms_relay)
 
             return carry
 
         lax.fori_loop(0, CHUNKS, chunk, 0)
+        if relayed:
+
+            @pl.when(is_last)
+            def _():
+                pass_on(iteration, terms_relay, terms_onward)
 
     def chain_rows(base, count, halves, total):
         parts_of = [transposed_dot(coupling[base + u], halves[u]) for u in range(count)]
@@ -427,7 +512,7 @@
                     return inner
 
                 loop(span, step)
-                bar_copy(iteration, c).start()
+                start_split(iteration, c, is_high, bar_copy, bar_relay)
 
             return carry
 
@@ -474,6 +559,12 @@
         more = iteration < ITERS - 1
         loop(blocks, gather_local, cost_t[...])
         answer_terms(iteration)
+        if relayed:
+
+            @pl.when(is_first)
+            def _():
+                pass_on(iteration, bar_relay, bar_onward)
+
         move_second(iteration)
         move_first(iteration)
         if iteration == 0:
@@ -501,6 +592,16 @@
         @pl.when(has_prev)
         def _():
             finish_sends(bar_copy, iteration)
+
+        if relayed:
+
+            @pl.when(is_last)
+            def _():
+                finish_onward(iteration, terms_onward)
+
+            @pl.when(is_first)
+            def _():
+                finish_onward(iteration, bar_onward)
 
     store_mu = pltpu.make_async_copy(mu, mu_out, store_sems.at[2])
     store_mu.start()
@@ -584,6 +685,8 @@
                 wide(slots, BF16),
                 wide(slots, BF16),
                 wide(slots, BF16),
+                wide(slots // 2, BF16),
+                wide(slots // 2, BF16),
                 wide(blocks, BF16),
                 wide(blocks, BF16),
                 pltpu.VMEM(block_shape, F32),
@@ -592,6 +695,8 @@
                 pltpu.VMEM((ITERS, scens) + block_shape, BF16),
                 sems((6,)),
                 sems((3,)),
+                sems((ITERS, CHUNKS)),
+                sems((ITERS, CHUNKS)),
                 sems((ITERS, CHUNKS)),
                 sems((ITERS, CHUNKS)),
                 sems((ITERS, CHUNKS)),

time: 108 us -> 99.1 us (0.918)
  the two profiles are of different devices: /device:TPU:1 before, /device:TPU:5 now
where the time goes in v3:
time: 99.1 us; the launch traced here: 98.8 us
  Pallas kernels  85.9 us (87%)
  local copies, waits for them, and re-layouts  10.9 us (11%)
  between operations  1.99 us (2%)
    pallas_call x1, Pallas kernels, call(): pl.pallas_call(kernel, out_shape=(jax.ShapeDtypeStruct((BLK, blocks), F32...  79.3 us
    unnamed x8, local copies, waits for them, and re-layouts  10.9 us
    pallas_call x1, Pallas kernels, body(): pl.pallas_call(functools.partial(prepare, few), out_shape=(jax.ShapeDtype...  6.57 us

profile of v3, /device:TPU:5, one launch (start us, length us, event | category | flops | bytes accessed | tf_op | source)
XLA Modules:
  0.0 98.8 jit_solution(3303103301325419624)
XLA Ops:
  1.3 6.6 %shard_map.174 = (s32[24,128]{1,0:T(8,128)S(1)}, s32[1,128]{1,0:T(1,128)}) custom-call(s32[1,128]{1,0:T(1,128)} %bitcast.21, s32[1,128]{1,0:T(1,128)} %bitcast.22, s32[4,96]{1,0:T(4,128)} %bitcast.20, s32[1,96]{1,0:T(1,128)} %bitcast.23, s32[1]{0:T(128)S(6)} %copy.31.count), custom_call_target="tpu_custom_call" | custom-call | tf_op jit(solution)/shard_map/pallas_call | solution.py:638
  8.5 79.4 %conditional.1 = ((f32[64,128]{1,0:T(8,128)S(1)}, f32[128,64,128]{2,1,0:T(8,128)}, f32[96,64,128]{2,1,0:T(8,128)}, f32[128,64,128]{2,1,0:T(8,128)})) conditional(s32[]{:T(128)} %bitcast.4, (s32[24,128]{1,0:T(8,128)S(1)}, f32[64,128]{1,0:T(8,128)}, f32[64,96]{1,0:T(8,128)}, f32[64,128]{1,0:T(8,128)}, f32[64,128]{1,0:T(8,128)}, ...), branch_computations={%region_0.0_spmd, %region_1.0_spmd} | conditional | flops 3200000000 | bytes 30000008 | solution.py:726
  8.6 79.3 %branch_0_fun.1 = (f32[64,128]{1,0:T(8,128)S(1)}, f32[128,64,128]{2,1,0:T(8,128)}, f32[96,64,128]{2,1,0:T(8,128)}, f32[128,64,128]{2,1,0:T(8,128)}) custom-call(s32[24,128]{1,0:T(8,128)S(1)} %get-tuple-element.44.index, f32[64,128]{1,0:T(8,128)} %get-tuple-element.45.cost_t, f32[64,96]{1,0:T(8,128)} %get-tuple-element.46.demand_t, ...), custom_call_target="tpu_custom_call" | custom-call | flops 3200000000 | bytes 30000000 | tf_op jit(solution)/shard_map/cond/branch_0_fun/pallas_call | solution.py:659
  87.9 0.6 copy.32
  88.5 0.0 copy-start.1
  88.5 4.9 %copy.33 = f32[128,64,128]{2,1,0:T(8,128)} copy(f32[128,64,128]{2,1,0:T(8,128)} %get-tuple-element.95) | data formatting | bytes 8388608
  93.5 0.0 copy-done.1
  93.5 0.0 copy-start
  93.5 1.7 %copy.34 = f32[96,64,128]{2,1,0:T(8,128)} copy(f32[96,64,128]{2,1,0:T(8,128)S(1)} %copy-done.1) | data formatting | bytes 6291456
  95.1 1.7 %copy-done = f32[128,64,128]{2,1,0:T(8,128)S(1)} copy-done((f32[128,64,128]{2,1,0:T(8,128)S(1)}, f32[128,64,128]{2,1,0:T(8,128)}, u32[]{:S(2)}) %copy-start) | copy-done | bytes 4194328
  96.8 2.0 %copy.35 = f32[128,64,128]{2,1,0:T(8,128)} copy(f32[128,64,128]{2,1,0:T(8,128)S(1)} %copy-done) | data formatting | bytes 8388608
Async XLA Ops:
  88.5 4.9 %copy-start.1 = (f32[96,64,128]{2,1,0:T(8,128)S(1)}, f32[96,64,128]{2,1,0:T(8,128)}, u32[]{:S(2)}) copy-start(f32[96,64,128]{2,1,0:T(8,128)} %get-tuple-element.96) | copy-start | bytes 9437188
  93.5 3.3 %copy-start = (f32[128,64,128]{2,1,0:T(8,128)S(1)}, f32[128,64,128]{2,1,0:T(8,128)}, u32[]{:S(2)}) copy-start(f32[128,64,128]{2,1,0:T(8,128)} %get-tuple-element.97) | copy-start | bytes 12582916
